TPU v7x, 32 devices: a whole 2x2x4 slice. The times are simulated.
32 devices in a mesh: fsdp: 8 (over y, x, core), tensor: 4 (over z).
Axes of the slice: x: 2, y: 2, z: 4, core: 2. Of those that a mesh axis runs over, the one named last changes fastest.
Arguments:
- inputs: bfloat16 [2, 4096, 768], P(None, ('fsdp', 'tensor')), may hold values from -6 to 6
- cotangent: bfloat16 [2, 4096, 768], P(None, ('fsdp', 'tensor')), may hold values from -6 to 6
- segment_ids: int32 [2, 4096], P(None, 'fsdp'), may hold values from 0 to 3, as said below
- qkv_weight: float32 [768, 3, 768], P('fsdp', None, 'tensor'), may hold values from -0.21875 to 0.21875
- qkv_first: float32 [768, 3, 768], P('fsdp', None, 'tensor')
- qkv_second: float32 [768, 3, 768], P('fsdp', None, 'tensor'), as said below
- out_weight: float32 [768, 768], P('tensor', 'fsdp'), may hold values from -1.75 to 1.75
- out_first: float32 [768, 768], P('tensor', 'fsdp')
- out_second: float32 [768, 768], P('tensor', 'fsdp'), as said below
- up_weight: float32 [768, 3072], P('fsdp', 'tensor'), may hold values from -0.21875 to 0.21875
- up_first: float32 [768, 3072], P('fsdp', 'tensor')
- up_second: float32 [768, 3072], P('fsdp', 'tensor'), as said below
- down_weight: float32 [3072, 768], P('tensor', 'fsdp'), may hold values from -0.109375 to 0.109375
- down_first: float32 [3072, 768], P('tensor', 'fsdp')
- down_second: float32 [3072, 768], P('tensor', 'fsdp'), as said below
- vectors: float32 [8, 768], replicated, as said below
- vectors_first: float32 [8, 768], replicated
- vectors_second: float32 [8, 768], replicated, as said below
- unit_bias: float32 [3072], replicated, may hold values from -4 to 4
- unit_bias_first: float32 [3072], replicated
- unit_bias_second: float32 [3072], replicated, as said below
Outputs:
- layer_output: bfloat16 [2, 4096, 768], P(None, ('fsdp', 'tensor'))
- input_grad: float32 [2, 4096, 768], P(None, ('fsdp', 'tensor'))
- qkv_updated: float32 [768, 3, 768], P('fsdp', None, 'tensor')
- qkv_first_new: float32 [768, 3, 768], P('fsdp', None, 'tensor')
- qkv_second_new: float32 [768, 3, 768], P('fsdp', None, 'tensor')
- out_updated: float32 [768, 768], P('tensor', 'fsdp')
- out_first_new: float32 [768, 768], P('tensor', 'fsdp')
- out_second_new: float32 [768, 768], P('tensor', 'fsdp')
- up_updated: float32 [768, 3072], P('fsdp', 'tensor')
- up_first_new: float32 [768, 3072], P('fsdp', 'tensor')
- up_second_new: float32 [768, 3072], P('fsdp', 'tensor')
- down_updated: float32 [3072, 768], P('tensor', 'fsdp')
- down_first_new: float32 [3072, 768], P('tensor', 'fsdp')
- down_second_new: float32 [3072, 768], P('tensor', 'fsdp')
- vectors_updated: float32 [8, 768], replicated
- vectors_first_new: float32 [8, 768], replicated
- vectors_second_new: float32 [8, 768], replicated
- unit_bias_updated: float32 [3072], replicated
- unit_bias_first_new: float32 [3072], replicated
- unit_bias_second_new: float32 [3072], replicated
Inputs may be any that keep to these rules, and one draw needn't show every extreme that they name: `segment_ids`: within each sequence of 512 positions the ids never fall and number its packed documents from 0; for each index of fsdp one of its 2 sequences is a single document. `vectors`: rows 4 and 6 are norms' gains, the other rows biases. `qkv_second`: Positive. `out_second`: Positive. `up_second`: Positive. `down_second`: Positive. `vectors_second`: Positive. `unit_bias_second`: Positive.
All inputs are finite; a program needn't handle non-finite values.
Results may differ from a plain program's by a relative error of at most 0.014.
The roundings to bfloat16 on the way count: a program that leaves them out, or rounds other values in their place, can miss the bound.
Values may be sent and summed in bfloat16 or wider, within the bound.
A program may use at most 128 MiB of HBM per device.

v0:
```python
import jax
import jax.numpy as jnp
from jax import lax
from jax.sharding import PartitionSpec as P

HD = 64
SEQ = 512
MICRO = 2
STEP = 3


EPSILON = 1e-05
NEGATIVE = -1000000000.0
LEARNING_RATES = (0.03, 0.2, 0.03, 0.015, 0.1, 0.1)
WEIGHT_DECAYS = (0.01, 0.01, 0.01, 0.01, 0.0, 0.0)


def contract(left, right, left_dim, right_dim):
    return lax.dot_general(
        left, right, (((left_dim,), (right_dim,)), ((), ())), preferred_element_type=jnp.float32
    )


def gather_rows(shard):
    return lax.all_gather(shard, "tensor", axis=0, tiled=True)


def reduce_rows(left, right, right_dim):
    return lax.psum_scatter(
        contract(left, right, 1, right_dim), "tensor", scatter_dimension=0, tiled=True
    )


def norm_forward(rows, gain, offset):
    center = rows - jnp.mean(rows, axis=1, keepdims=True)
    inverse = lax.rsqrt(jnp.mean(center * center, axis=1, keepdims=True) + EPSILON)
    normed = center * inverse
    return (normed * gain + offset, normed, inverse)


def norm_backward(grad_out, normed, inverse, gain):
    scaled = grad_out * gain
    grad_rows = inverse * (
        scaled
        - jnp.mean(scaled, axis=1, keepdims=True)
        - normed * jnp.mean(scaled * normed, axis=1, keepdims=True)
    )
    return (grad_rows, jnp.sum(grad_out * normed, axis=0), jnp.sum(grad_out, axis=0))


def masked_scores(queries, key_rows, segment_row):
    scores = contract(queries, key_rows, 1, 1) * HD ** (-0.5)
    same_doc = segment_row[:, None] == segment_row[None, :]
    return jnp.where(same_doc, scores, NEGATIVE)


def attend_forward(item):
    queries, key_rows, value_rows, segment_row = item
    scores = masked_scores(queries, key_rows, segment_row)
    top_score = jnp.max(scores, axis=1, keepdims=True)
    expos = jnp.exp(scores - top_score)
    totals = jnp.sum(expos, axis=1, keepdims=True)
    probs = expos / totals
    context = jnp.dot(probs.astype(jnp.bfloat16), value_rows, preferred_element_type=jnp.float32)
    return (context, top_score + jnp.log(totals))


def attend_backward(item):
    queries, key_rows, value_rows, segment_row, log_total, grad_context = item
    scores = masked_scores(queries, key_rows, segment_row)
    probs = jnp.exp(scores - log_total)
    grad_probs = contract(grad_context, value_rows, 1, 1)
    inner = jnp.sum(probs * grad_probs, axis=1, keepdims=True)
    grad_scores = (probs * (grad_probs - inner)).astype(jnp.bfloat16)
    scale_factor = HD ** (-0.5)
    grad_query = (
        jnp.dot(grad_scores, key_rows, preferred_element_type=jnp.float32) * scale_factor
    ).astype(jnp.bfloat16)
    grad_key = (contract(grad_scores, queries, 0, 0) * scale_factor).astype(jnp.bfloat16)
    grad_value = contract(probs.astype(jnp.bfloat16), grad_context, 0, 0).astype(jnp.bfloat16)
    return (grad_query, grad_key, grad_value)


def adam_update(master, moment_one, moment_two, gradient, step_rate, decay_rate):
    one_new = 0.9 * moment_one + 0.1 * gradient
    two_new = 0.999 * moment_two + 0.001 * gradient * gradient
    one_hat = one_new / (1.0 - 0.9**STEP)
    two_hat = two_new / (1.0 - 0.999**STEP)
    updated = master - step_rate * (one_hat / (jnp.sqrt(two_hat) + 1e-08) + decay_rate * master)
    return (updated, one_new, two_new)


def shards(
    inputs,
    cotangent,
    segment_ids,
    qkv_weight,
    qkv_first,
    qkv_second,
    out_weight,
    out_first,
    out_second,
    up_weight,
    up_first,
    up_second,
    down_weight,
    down_first,
    down_second,
    vectors,
    vectors_first,
    vectors_second,
    unit_bias,
    unit_bias_first,
    unit_bias_second,
):
    tensor_rank = lax.axis_index("tensor")
    head_width = qkv_weight.shape[2]
    unit_width = up_weight.shape[1]
    local_heads = head_width // HD
    head_start = tensor_rank * head_width
    unit_start = tensor_rank * unit_width
    query_bias = lax.dynamic_slice_in_dim(vectors[0], head_start, head_width, 0)
    value_bias = lax.dynamic_slice_in_dim(vectors[1], head_start, head_width, 0)
    unit_slice = lax.dynamic_slice_in_dim(unit_bias, unit_start, unit_width, 0)
    qkv_low = qkv_weight.astype(jnp.bfloat16)
    out_low = out_weight.astype(jnp.bfloat16)
    up_low = up_weight.astype(jnp.bfloat16)
    down_low = down_weight.astype(jnp.bfloat16)

    def to_items(rows):
        return rows.reshape(-1, SEQ, local_heads, HD).transpose(0, 2, 1, 3).reshape(-1, SEQ, HD)

    def from_items(items):
        return (
            items.reshape(-1, local_heads, SEQ, HD)
            .transpose(0, 2, 1, 3)
            .reshape(-1, local_heads * HD)
        )

    grad_totals = None
    vector_grad = jnp.zeros(vectors.shape, jnp.float32)
    unit_grad = jnp.zeros(unit_bias.shape, jnp.float32)
    output_rows = []
    input_rows = []
    for micro_step in range(MICRO):
        current = (
            lax.all_gather(qkv_low, "fsdp", axis=0, tiled=True),
            lax.all_gather(out_low, "fsdp", axis=1, tiled=True),
            lax.all_gather(up_low, "fsdp", axis=0, tiled=True),
            lax.all_gather(down_low, "fsdp", axis=1, tiled=True),
        )
        qkv_full, out_full, up_full, down_full = current
        qkv_flat = qkv_full.reshape(qkv_full.shape[0], 3 * head_width)
        local_rows = inputs[micro_step]
        whole_rows = gather_rows(local_rows)
        seq_rows = whole_rows.shape[0]
        mixed = jnp.dot(whole_rows, qkv_flat, preferred_element_type=jnp.float32).reshape(
            seq_rows, 3, head_width
        )
        queries = (mixed[:, 0] + query_bias).astype(jnp.bfloat16)
        key_rows = mixed[:, 1].astype(jnp.bfloat16)
        value_rows = (mixed[:, 2] + value_bias).astype(jnp.bfloat16)
        segment_items = jnp.repeat(segment_ids[micro_step].reshape(-1, SEQ), local_heads, axis=0)
        query_items = to_items(queries)
        key_items = to_items(key_rows)
        value_items = to_items(value_rows)
        context_items, log_items = lax.map(
            attend_forward, (query_items, key_items, value_items, segment_items)
        )
        context_low = from_items(context_items).astype(jnp.bfloat16)
        branch = reduce_rows(context_low, out_full, 0)
        residual_one = local_rows.astype(jnp.float32) + branch + vectors[2]
        first_norm, normed_one, inverse_one = norm_forward(residual_one, vectors[4], vectors[5])
        first_whole = gather_rows(first_norm.astype(jnp.bfloat16))
        hidden = jnp.dot(first_whole, up_full, preferred_element_type=jnp.float32) + unit_slice
        active_float, gelu_pull = jax.vjp(
            lambda pre_act: jax.nn.gelu(pre_act, approximate=False), hidden
        )
        active = active_float.astype(jnp.bfloat16)
        second = reduce_rows(active, down_full, 0)
        residual_two = first_norm + second + vectors[3]
        result_rows, normed_two, inverse_two = norm_forward(residual_two, vectors[6], vectors[7])
        output_rows.append(result_rows.astype(jnp.bfloat16))
        back_rows = cotangent[micro_step].astype(jnp.float32)
        grad_two, gain_two_grad, offset_two_grad = norm_backward(
            back_rows, normed_two, inverse_two, vectors[6]
        )
        down_bias_grad = jnp.sum(grad_two, axis=0)
        grad_branch_two = gather_rows(grad_two.astype(jnp.bfloat16))
        down_grad = contract(active, grad_branch_two, 0, 0)
        grad_active = contract(grad_branch_two, down_full, 1, 1)
        grad_hidden = gelu_pull(grad_active)[0].astype(jnp.bfloat16)
        unit_part = jnp.sum(grad_hidden.astype(jnp.float32), axis=0)
        up_grad = contract(first_whole, grad_hidden, 0, 0)
        grad_first = grad_two + reduce_rows(grad_hidden, up_full, 1)
        grad_one, gain_one_grad, offset_one_grad = norm_backward(
            grad_first, normed_one, inverse_one, vectors[4]
        )
        out_bias_grad = jnp.sum(grad_one, axis=0)
        grad_branch_one = gather_rows(grad_one.astype(jnp.bfloat16))
        out_grad = contract(context_low, grad_branch_one, 0, 0)
        grad_context = contract(grad_branch_one, out_full, 1, 1).astype(jnp.bfloat16)
        grad_query, grad_key, grad_value = lax.map(
            attend_backward,
            (query_items, key_items, value_items, segment_items, log_items, to_items(grad_context)),
        )
        query_grad_rows = from_items(grad_query)
        value_grad_rows = from_items(grad_value)
        grad_mixed = jnp.stack(
            [query_grad_rows, from_items(grad_key), value_grad_rows], axis=1
        ).reshape(seq_rows, 3 * head_width)
        qkv_grad = contract(whole_rows, grad_mixed, 0, 0).reshape(qkv_full.shape)
        input_part = grad_one + reduce_rows(grad_mixed, qkv_flat, 1)
        input_rows.append(input_part)
        zero_width = jnp.zeros((vectors.shape[1],), jnp.float32)
        query_bias_grad = lax.dynamic_update_slice_in_dim(
            zero_width, jnp.sum(query_grad_rows.astype(jnp.float32), axis=0), head_start, 0
        )
        value_bias_grad = lax.dynamic_update_slice_in_dim(
            zero_width, jnp.sum(value_grad_rows.astype(jnp.float32), axis=0), head_start, 0
        )
        vector_grad = vector_grad + jnp.stack(
            [
                query_bias_grad,
                value_bias_grad,
                out_bias_grad,
                down_bias_grad,
                gain_one_grad,
                offset_one_grad,
                gain_two_grad,
                offset_two_grad,
            ],
            axis=0,
        )
        unit_grad = unit_grad + lax.dynamic_update_slice_in_dim(
            jnp.zeros(unit_bias.shape, jnp.float32), unit_part, unit_start, 0
        )
        reduced = (
            lax.psum_scatter(qkv_grad, "fsdp", scatter_dimension=0, tiled=True),
            lax.psum_scatter(out_grad, "fsdp", scatter_dimension=1, tiled=True),
            lax.psum_scatter(up_grad, "fsdp", scatter_dimension=0, tiled=True),
            lax.psum_scatter(down_grad, "fsdp", scatter_dimension=1, tiled=True),
        )
        if grad_totals is None:
            grad_totals = reduced
        else:
            grad_totals = tuple((before + after for before, after in zip(grad_totals, reduced)))
    vector_total, unit_total = lax.psum((vector_grad, unit_grad), ("fsdp", "tensor"))
    masters = (qkv_weight, out_weight, up_weight, down_weight, vectors, unit_bias)
    firsts = (qkv_first, out_first, up_first, down_first, vectors_first, unit_bias_first)
    seconds = (qkv_second, out_second, up_second, down_second, vectors_second, unit_bias_second)
    gradients = (
        grad_totals[0],
        grad_totals[1],
        grad_totals[2],
        grad_totals[3],
        vector_total,
        unit_total,
    )
    news = [
        adam_update(
            masters[place],
            firsts[place],
            seconds[place],
            gradients[place],
            LEARNING_RATES[place],
            WEIGHT_DECAYS[place],
        )
        for place in range(6)
    ]
    layer_output = jnp.stack(output_rows, axis=0)
    input_grad = jnp.stack(input_rows, axis=0)
    return (
        layer_output,
        input_grad,
        news[0][0],
        news[0][1],
        news[0][2],
        news[1][0],
        news[1][1],
        news[1][2],
        news[2][0],
        news[2][1],
        news[2][2],
        news[3][0],
        news[3][1],
        news[3][2],
        news[4][0],
        news[4][1],
        news[4][2],
        news[5][0],
        news[5][1],
        news[5][2],
    )


def solution(mesh):
    placed = (
        P(None, ("fsdp", "tensor"), None),
        P(None, ("fsdp", "tensor"), None),
        P(None, "fsdp"),
        P("fsdp", None, "tensor"),
        P("fsdp", None, "tensor"),
        P("fsdp", None, "tensor"),
        P("tensor", "fsdp"),
        P("tensor", "fsdp"),
        P("tensor", "fsdp"),
        P("fsdp", "tensor"),
        P("fsdp", "tensor"),
        P("fsdp", "tensor"),
        P("tensor", "fsdp"),
        P("tensor", "fsdp"),
        P("tensor", "fsdp"),
        P(),
        P(),
        P(),
        P(),
        P(),
        P(),
    )
    return jax.shard_map(
        shards,
        mesh=mesh,
        in_specs=placed,
        out_specs=(
            P(None, ("fsdp", "tensor"), None),
            P(None, ("fsdp", "tensor"), None),
            P("fsdp", None, "tensor"),
            P("fsdp", None, "tensor"),
            P("fsdp", None, "tensor"),
            P("tensor", "fsdp"),
            P("tensor", "fsdp"),
            P("tensor", "fsdp"),
            P("fsdp", "tensor"),
            P("fsdp", "tensor"),
            P("fsdp", "tensor"),
            P("tensor", "fsdp"),
            P("tensor", "fsdp"),
            P("tensor", "fsdp"),
            P(),
            P(),
            P(),
            P(),
            P(),
            P(),
        ),
        check_vma=False,
    )
```

profile of v0, /device:TPU:9, one launch (start us, length us, event | category | flops | bytes accessed | tf_op | source)
XLA Modules:
  0.0 643.1 jit_solution(14019371769345004570)
XLA Ops:
  9.1 12.2 %all_gather.41 = bf16[768,3,192]{2,0,1:T(8,128)(2,1)S(1)} all-gather(bf16[96,3,192]{2,0,1:T(8,128)(2,1)S(1)} %convert_element_type.217), channel_id=1, replica_groups=mesh['fsdp'=8,'tensor'=4] {'fsdp'}, dimensions={0}, use_global_device_ids=true | all-gather | bytes 995328 | tf_op jit(solution)/shard_map/all_gather | solution.py:147
  22.7 16.9 %all-gather.1 = bf16[1,512,768]{2,1,0:T(8,128)(2,1)S(1)} all-gather(bf16[1,128,768]{2,1,0:T(8,128)(2,1)S(1)} %get-tuple-element.372), channel_id=3, replica_groups=mesh['fsdp'=8,'tensor'=4] {'tensor'}, dimensions={1}, use_global_device_ids=true | all-gather | bytes 983040 | tf_op jit(solution)/shard_map/all_gather | solution.py:25
  43.2 16.3 %all-gather = bf16[1,512,768]{2,1,0:T(8,128)(2,1)S(1)} all-gather(bf16[1,128,768]{2,1,0:T(8,128)(2,1)S(1)} %copy-done.42), channel_id=2, replica_groups=mesh['fsdp'=8,'tensor'=4] {'tensor'}, dimensions={1}, use_global_device_ids=true | all-gather | bytes 983040 | tf_op jit(solution)/shard_map/all_gather | solution.py:25
  71.6 6.5 %while.53 = (s32[]{:T(128)}, bf16[3,512,64]{1,2,0:T(8,128)(2,1)S(1)}, f32[3,512,1]{1,2,0:T(1,128)}, s32[3,512]{1,0:T(4,128)}, bf16[3,512,64]{2,1,0:T(8,128)(2,1)...) while((s32[]{:T(128)}, bf16[3,512,64]{1,2,0:T(8,128)(2,1)S(1)}, ...), condition=%wide.region_13.14_spmd, body=%wide.region_10.13_spmd.sunk | while | flops 69467648 | bytes 3701337 | solution.py:167
  79.0 12.0 %all_gather.42 = bf16[192,768]{0,1:T(8,128)(2,1)S(1)} all-gather(bf16[192,96]{0,1:T(8,128)(2,1)S(1)} %copy.64), channel_id=1, replica_groups=mesh['fsdp'=8,'tensor'=4] {'fsdp'}, dimensions={1}, use_global_device_ids=true | all-gather | bytes 331776 | tf_op jit(solution)/shard_map/all_gather | solution.py:148
  94.0 5.4 while.52
  104.6 21.3 %reduce-scatter.19.cloned.1.call-done = f32[128,768]{1,0:T(8,128)} async-done(((f32[512,768]{1,0:T(8,128)}), f32[128,768]{1,0:T(8,128)}) %reduce-scatter.19.cloned.1.call-update) | async-done | bytes 393232 | tf_op jit(solution)/shard_map/reduce_scatter | solution.py:29
  125.9 36.6 %reduce-scatter.15.cloned.1.call-done = f32[128,768]{1,0:T(8,128)} async-done(((f32[512,768]{1,0:T(8,128)}), f32[128,768]{1,0:T(8,128)}) %reduce-scatter.15.cloned.1.call-update) | async-done | bytes 393232 | tf_op jit(solution)/shard_map/reduce_scatter | solution.py:29
  166.1 15.9 %all_gather.47 = bf16[512,768]{1,0:T(8,128)(2,1)} all-gather(bf16[128,768]{1,0:T(8,128)(2,1)S(1)} %get-tuple-element.384), channel_id=1, replica_groups=mesh['fsdp'=8,'tensor'=4] {'tensor'}, dimensions={0}, use_global_device_ids=true | all-gather | bytes 983040 | tf_op jit(solution)/shard_map/all_gather | solution.py:25
  182.0 7.2 %multiply_convert_fusion.2 = (bf16[512,768]{1,0:T(8,128)(2,1)}, f32[512,768]{1,0:T(8,128)}, f32[512,768]{1,0:T(8,128)}) fusion(f32[768]{0:T(1024)} %dynamic_slice.74, bf16[512,768]{1,0:T(8,128)(2,1)} %all_gather.47, bf16[768,768]{1,0:T(8,128)(2,1)} %all-gather.5.cloned.1.call-done), kind=kOutput, calls=%fused_computation.126 | convolution fusion | flops 629932032 | bytes 5901312 | tf_op jit(solution)/shard_map/dot_general | solution.py:175
  189.2 3.5 fusion.171
  192.8 18.6 %all_gather.43 = bf16[512,768]{1,0:T(8,128)(2,1)S(1)} all-gather(bf16[128,768]{1,0:T(8,128)(2,1)} %get-tuple-element.383), channel_id=1, replica_groups=mesh['fsdp'=8,'tensor'=4] {'tensor'}, dimensions={0}, use_global_device_ids=true | all-gather | bytes 983040 | tf_op jit(solution)/shard_map/all_gather | solution.py:25
  211.4 6.7 %multiply_convert_fusion.3 = (bf16[512,768]{1,0:T(8,128)(2,1)S(1)}, f32[512,768]{1,0:T(8,128)}, f32[512,768]{1,0:T(8,128)}) fusion(f32[768]{0:T(1024)} %dynamic_slice.74, bf16[512,768]{1,0:T(8,128)(2,1)S(1)} %all_gather.43, bf16[768,768]{1,0:T(8,128)(2,1)} %all-gather.5.cloned.1.call-done), kind=kOutput, calls=%fused_computation.139 | convolution fusion | flops 629932032 | bytes 5901312 | tf_op jit(solution)/shard_map/dot_general | solution.py:175
  221.1 15.8 %reduce-scatter.21.cloned.1.call-done = f32[128,768]{1,0:T(8,128)} async-done(((f32[512,768]{1,0:T(8,128)}), f32[128,768]{1,0:T(8,128)}) %reduce-scatter.21.cloned.1.call-update) | async-done | bytes 393232 | tf_op jit(solution)/shard_map/reduce_scatter | solution.py:29
  236.9 37.4 %reduce-scatter.17.cloned.1.call-done = f32[128,768]{1,0:T(8,128)} async-done(((f32[512,768]{1,0:T(8,128)}), f32[128,768]{1,0:T(8,128)}) %reduce-scatter.17.cloned.1.call-update) | async-done | bytes 393232 | tf_op jit(solution)/shard_map/reduce_scatter | solution.py:29
  280.3 15.7 %all_gather.48 = bf16[512,768]{1,0:T(8,128)(2,1)S(1)} all-gather(bf16[128,768]{1,0:T(8,128)(2,1)S(1)} %convert_element_type.244), channel_id=1, replica_groups=mesh['fsdp'=8,'tensor'=4] {'tensor'}, dimensions={0}, use_global_device_ids=true | all-gather | bytes 983040 | tf_op jit(solution)/shard_map/all_gather | solution.py:25
  301.8 22.0 %all_gather.50 = bf16[512,768]{1,0:T(8,128)(2,1)S(1)} all-gather(bf16[128,768]{1,0:T(8,128)(2,1)S(1)} %convert_element_type.250), channel_id=1, replica_groups=mesh['fsdp'=8,'tensor'=4] {'tensor'}, dimensions={0}, use_global_device_ids=true | all-gather | bytes 983040 | tf_op jit(solution)/shard_map/all_gather | solution.py:25
  323.8 4.0 convert_reduce_fusion
  330.7 2.3 fusion.176
  340.1 6.2 reduce-scatter.23.cloned.1.call-done
  346.3 2.6 multiply_reduce_fusion.3
  350.0 33.5 %reduce-scatter.27.cloned.1.call-done = f32[128,768]{1,0:T(8,128)} async-done(((f32[512,768]{1,0:T(8,128)}), f32[128,768]{1,0:T(8,128)}) %reduce-scatter.27.cloned.1.call-update) | async-done | bytes 393232 | tf_op jit(solution)/shard_map/reduce_scatter | solution.py:29
  385.8 15.8 %all_gather.49 = bf16[512,768]{1,0:T(8,128)(2,1)S(1)} all-gather(bf16[128,768]{1,0:T(8,128)(2,1)S(1)} %convert_element_type.246), channel_id=1, replica_groups=mesh['fsdp'=8,'tensor'=4] {'tensor'}, dimensions={0}, use_global_device_ids=true | all-gather | bytes 983040 | tf_op jit(solution)/shard_map/all_gather | solution.py:25
  404.6 15.5 %all_gather.51 = bf16[512,768]{1,0:T(8,128)(2,1)S(1)} all-gather(bf16[128,768]{1,0:T(8,128)(2,1)S(1)} %convert_element_type.252), channel_id=1, replica_groups=mesh['fsdp'=8,'tensor'=4] {'tensor'}, dimensions={0}, use_global_device_ids=true | all-gather | bytes 983040 | tf_op jit(solution)/shard_map/all_gather | solution.py:25
  424.5 18.2 %while.55 = (s32[]{:T(128)}, bf16[3,512,64]{1,2,0:T(8,128)(2,1)}, bf16[3,512,64]{1,2,0:T(8,128)(2,1)}, bf16[3,512,64]{1,2,0:T(8,128)(2,1)}, s32[3,512]{1,0:T(4,1...) while((s32[]{:T(128)}, bf16[3,512,64]{1,2,0:T(8,128)(2,1)}, ...), condition=%wide.region_36.37_spmd, body=%wide.region_34.36_spmd.sunk | while | flops 170556928 | bytes 9002101 | solution.py:203
  443.9 2.4 convolution_add_fusion.5
  448.6 10.5 %while.54 = (s32[]{:T(128)}, bf16[3,512,64]{1,2,0:T(8,128)(2,1)S(1)}, bf16[3,512,64]{1,2,0:T(8,128)(2,1)S(1)}, bf16[3,512,64]{1,2,0:T(8,128)(2,1)S(1)}, s32[3,51...) while((s32[]{:T(128)}, ...), condition=%wide.region_27.28_spmd, body=%wide.region_25.27_spmd.sunk | while | flops 170556928 | bytes 9002101 | solution.py:203
  468.1 3.0 convolution_bitcast_fusion.2
  476.7 45.0 %all-reduce = (f32[8,768]{1,0:T(8,128)S(1)}, f32[3072]{0:T(1024)S(1)}) all-reduce(f32[8,768]{1,0:T(8,128)S(1)} %add.459, f32[3072]{0:T(1024)S(1)} %add_dynamic-update-slice_fusion), channel_id=1, replica_groups=mesh['fsdp'=8,'tensor'=4] {'fsdp','tensor'}, use_global_device_ids=true, to_apply=%region_62.63 | all-reduce | flops 9216 | bytes 73728 | tf_op jit(solution)/shard_map/psum | solution.py:248
  529.1 31.8 %reduce-scatter.31.cloned.1.call-done = f32[96,3,192]{2,0,1:T(8,128)} async-done(((f32[768,3,192]{2,0,1:T(8,128)}), f32[96,3,192]{2,0,1:T(8,128)}) %reduce-scatter.31.cloned.1.call-update) | async-done | bytes 221200 | tf_op jit(solution)/shard_map/reduce_scatter | solution.py:239
  562.9 33.8 %reduce-scatter.25.cloned.1.call-done = f32[128,768]{1,0:T(8,128)} async-done(((f32[512,768]{1,0:T(8,128)}), f32[128,768]{1,0:T(8,128)}) %reduce-scatter.25.cloned.1.call-update) | async-done | bytes 393232 | tf_op jit(solution)/shard_map/reduce_scatter | solution.py:29
  597.8 35.5 %reduce-scatter.29.cloned.1.call-done = f32[128,768]{1,0:T(8,128)} async-done(((f32[512,768]{1,0:T(8,128)}), f32[128,768]{1,0:T(8,128)}) %reduce-scatter.29.cloned.1.call-update) | async-done | bytes 393232 | tf_op jit(solution)/shard_map/reduce_scatter | solution.py:29
  (431 shorter events, 136.1 us)
Async XLA Ops:
  8.0 117.9 %reduce-scatter.19.cloned.1.call-start = ((), (), s32[]{:S(2)}) async-start(), calls=%async_computation.16 | async-start | bytes 1966080 | tf_op jit(solution)/shard_map/reduce_scatter | solution.py:29
  92.6 69.9 %reduce-scatter.15.cloned.1.call-start = ((), (), s32[]{:S(2)}) async-start(), calls=%async_computation.12 | async-start | bytes 1966080 | tf_op jit(solution)/shard_map/reduce_scatter | solution.py:29
  101.6 80.4 %all-gather.5.cloned.1.call-start = ((), (), s32[]{:S(2)}) async-start(), calls=%async_computation.13 | async-start | bytes 1327104 | tf_op jit(solution)/shard_map/all_gather | solution.py:149
  102.3 86.9 %all-gather.7.cloned.1.call-start = ((), (), s32[]{:S(2)}) async-start(), calls=%async_computation.14 | async-start | bytes 1327104 | tf_op jit(solution)/shard_map/all_gather | solution.py:150
  103.2 133.7 %reduce-scatter.21.cloned.1.call-start = ((), (), s32[]{:S(2)}) async-start(), calls=%async_computation.17 | async-start | bytes 1966080 | tf_op jit(solution)/shard_map/reduce_scatter | solution.py:29
  192.7 81.6 %reduce-scatter.17.cloned.1.call-start = ((), (), s32[]{:S(2)}) async-start(), calls=%async_computation.15 | async-start | bytes 1966080 | tf_op jit(solution)/shard_map/reduce_scatter | solution.py:29
  221.1 125.2 %reduce-scatter.23.cloned.1.call-start = ((), (), s32[]{:S(2)}) async-start(), calls=%async_computation.18 | async-start | bytes 1966080 | tf_op jit(solution)/shard_map/reduce_scatter | solution.py:29
  300.7 82.8 %reduce-scatter.27.cloned.1.call-start = ((), (), s32[]{:S(2)}) async-start(), calls=%async_computation.20 | async-start | bytes 1966080 | tf_op jit(solution)/shard_map/reduce_scatter | solution.py:29
  300.7 23.1 %copy-start.86 = (bf16[768,768]{0,1:T(8,128)(2,1)S(1)}, bf16[768,768]{0,1:T(8,128)(2,1)}, u32[]{:S(2)}) copy-start(bf16[768,768]{0,1:T(8,128)(2,1)} %all-gather.7.cloned.1.call-done) | copy-start | bytes 3538948
  330.7 192.3 %reduce-scatter.35.cloned.1.call-start = ((), (), s32[]{:S(2)}) async-start(), calls=%async_computation.24 | async-start | bytes 2654208 | tf_op jit(solution)/shard_map/reduce_scatter | solution.py:242
  335.4 189.7 %reduce-scatter.33.cloned.1.call-start = ((), (), s32[]{:S(2)}) async-start(), calls=%async_computation.23 | async-start | bytes 2654208 | tf_op jit(solution)/shard_map/reduce_scatter | solution.py:241
  340.0 187.2 %reduce-scatter.37.cloned.1.call-start = ((), (), s32[]{:S(2)}) async-start(), calls=%async_computation.25 | async-start | bytes 884736
  459.2 101.7 %reduce-scatter.31.cloned.1.call-start = ((), (), s32[]{:S(2)}) async-start(), calls=%async_computation.22 | async-start | bytes 2654208 | tf_op jit(solution)/shard_map/reduce_scatter | solution.py:239
  463.7 133.0 %reduce-scatter.25.cloned.1.call-start = ((), (), s32[]{:S(2)}) async-start(), calls=%async_computation.19 | async-start | bytes 1966080 | tf_op jit(solution)/shard_map/reduce_scatter | solution.py:29
  467.1 166.2 %reduce-scatter.29.cloned.1.call-start = ((), (), s32[]{:S(2)}) async-start(), calls=%async_computation.21 | async-start | bytes 1966080 | tf_op jit(solution)/shard_map/reduce_scatter | solution.py:29
  472.0 49.7 %copy-start.59 = (f32[3072]{0:T(1024)S(1)}, f32[3072]{0:T(1024)}, u32[]{:S(2)}) copy-start(f32[3072]{0:T(1024)} %param.47) | copy-start | bytes 36868
  472.0 49.7 %copy-start.73 = (f32[3072]{0:T(1024)S(1)}, f32[3072]{0:T(1024)}, u32[]{:S(2)}) copy-start(f32[3072]{0:T(1024)} %param.48) | copy-start | bytes 36868
  472.0 49.7 %copy-start.74 = (f32[3072]{0:T(1024)S(1)}, f32[3072]{0:T(1024)}, u32[]{:S(2)}) copy-start(f32[3072]{0:T(1024)} %param.49) | copy-start | bytes 36868
  472.0 50.3 %copy-start.53 = (f32[8,768]{1,0:T(8,128)S(1)}, f32[8,768]{1,0:T(8,128)}, u32[]{:S(2)}) copy-start(f32[8,768]{1,0:T(8,128)} %param.44) | copy-start | bytes 73732
  472.0 50.3 %copy-start.57 = (f32[8,768]{1,0:T(8,128)S(1)}, f32[8,768]{1,0:T(8,128)}, u32[]{:S(2)}) copy-start(f32[8,768]{1,0:T(8,128)} %param.45) | copy-start | bytes 73732
  472.0 50.3 %copy-start.58 = (f32[8,768]{1,0:T(8,128)S(1)}, f32[8,768]{1,0:T(8,128)}, u32[]{:S(2)}) copy-start(f32[8,768]{1,0:T(8,128)} %param.46) | copy-start | bytes 73732
  472.0 50.9 %copy-start.29 = (f32[768,96]{0,1:T(8,128)S(1)}, f32[768,96]{0,1:T(8,128)}, u32[]{:S(2)}) copy-start(f32[768,96]{0,1:T(8,128)} %param.41) | copy-start | bytes 884740
  472.1 50.9 %copy-start.46 = (f32[768,96]{0,1:T(8,128)S(1)}, f32[768,96]{0,1:T(8,128)}, u32[]{:S(2)}) copy-start(f32[768,96]{0,1:T(8,128)} %param.42) | copy-start | bytes 884740
  472.1 50.9 %copy-start.47 = (f32[768,96]{0,1:T(8,128)S(1)}, f32[768,96]{0,1:T(8,128)}, u32[]{:S(2)}) copy-start(f32[768,96]{0,1:T(8,128)} %param.43) | copy-start | bytes 884740
  473.7 51.3 %copy-start.31 = (f32[96,768]{1,0:T(8,128)S(1)}, f32[96,768]{1,0:T(8,128)}, u32[]{:S(2)}) copy-start(f32[96,768]{1,0:T(8,128)} %param.38) | copy-start | bytes 884740
  473.7 51.3 %copy-start.48 = (f32[96,768]{1,0:T(8,128)S(1)}, f32[96,768]{1,0:T(8,128)}, u32[]{:S(2)}) copy-start(f32[96,768]{1,0:T(8,128)} %param.39) | copy-start | bytes 884740
  473.7 51.4 %copy-start.49 = (f32[96,768]{1,0:T(8,128)S(1)}, f32[96,768]{1,0:T(8,128)}, u32[]{:S(2)}) copy-start(f32[96,768]{1,0:T(8,128)} %param.40) | copy-start | bytes 884740
  525.0 35.9 %copy-start.32 = (f32[96,3,192]{2,0,1:T(8,128)S(1)}, f32[96,3,192]{2,0,1:T(8,128)}, u32[]{:S(2)}) copy-start(f32[96,3,192]{2,0,1:T(8,128)} %param.32) | copy-start | bytes 663556
  525.0 35.9 %copy-start.50 = (f32[96,3,192]{2,0,1:T(8,128)S(1)}, f32[96,3,192]{2,0,1:T(8,128)}, u32[]{:S(2)}) copy-start(f32[96,3,192]{2,0,1:T(8,128)} %param.33) | copy-start | bytes 663556
  525.0 35.9 %copy-start.51 = (f32[96,3,192]{2,0,1:T(8,128)S(1)}, f32[96,3,192]{2,0,1:T(8,128)}, u32[]{:S(2)}) copy-start(f32[96,3,192]{2,0,1:T(8,128)} %param.34) | copy-start | bytes 663556
  527.2 69.5 %copy-start.13 = (f32[128,768]{1,0:T(8,128)S(1)}, f32[128,768]{1,0:T(8,128)}, u32[]{:S(2)}) copy-start(f32[128,768]{1,0:T(8,128)} %copy-done.12) | copy-start | bytes 1179652
  529.1 104.2 %copy-start.11 = (f32[128,768]{1,0:T(8,128)S(1)}, f32[128,768]{1,0:T(8,128)}, u32[]{:S(2)}) copy-start(f32[128,768]{1,0:T(8,128)} %copy-done.10) | copy-start | bytes 1179652
  (71 other events, 328.2 us)
Sparse Core Ops, SparseCore 0:
  92.7 33.1 reduce-scatter.18
  128.2 34.2 reduce-scatter.14
  192.8 44.0 reduce-scatter.20
  239.1 35.1 reduce-scatter.16
  300.8 45.4 reduce-scatter.22
  348.5 34.9 reduce-scatter.26
  386.8 43.3 reduce-scatter.34
  433.9 42.4 reduce-scatter.32
  480.2 34.6 reduce-scatter.36
  518.1 42.7 reduce-scatter.30
  563.3 33.3 reduce-scatter.24
  599.0 34.2 reduce-scatter.28
Sparse Core Ops, SparseCore 1:
  104.5 24.0 all-gather.4
  130.9 23.9 all-gather.6
where the time goes:
time: 654 us; the launch traced here: 643 us
  waiting for transfers between devices  252 us (39%)
  blocking collectives  206 us (31%)
  matrix products  82 us (13%)
  local copies, waits for them, and re-layouts  45.5 us (7%)
  other arithmetic  39.2 us (6%)
  between operations  17.3 us (3%)
    reduce_scatter x8, waiting for transfers between devices, reduce_rows(): lax.psum_scatter(contract(left, right, 1, right_dim), 'tensor', scatter_d...  220 us
    all_gather x8, blocking collectives, gather_rows(): return lax.all_gather(shard, 'tensor', axis=0, tiled=True)  137 us
    dot_general x50, matrix products, contract(): lax.dot_general(left, right, (((left_dim,), (right_dim,)), ((), ())), pre...  58.8 us
    psum x1, blocking collectives, shards(): lax.psum((vector_grad, unit_grad), ('fsdp', 'tensor'))  45 us
    reduce_scatter x1, waiting for transfers between devices, shards(): lax.psum_scatter(qkv_grad, 'fsdp', scatter_dimension=0, tiled=True)  31.8 us
    dot_general x2, matrix products, shards(): jnp.dot(first_whole, up_full, preferred_element_type=jnp.float32)  14 us
  transfers between devices with their start and end apart: 14, of which 9 were waited for; matrix products, arithmetic and copies ran while one was open for 18% of the time, Pallas kernels for 0%

commit v1 on v0

v1 whole, which is shorter than its diff:
```python
import jax
import jax.numpy as jnp
from jax import lax
from jax.experimental import pallas as pl
from jax.experimental.pallas import tpu as pltpu
from jax.sharding import PartitionSpec as P

HD = 64
SEQ = 512
MICRO = 2
STEP = 3


EPSILON = 1e-05
NEGATIVE = -1000000000.0
LEARNING_RATES = (0.03, 0.2, 0.03, 0.015, 0.1, 0.1)
WEIGHT_DECAYS = (0.01, 0.01, 0.01, 0.01, 0.0, 0.0)


def contract(left, right, left_dim, right_dim):
    return lax.dot_general(
        left, right, (((left_dim,), (right_dim,)), ((), ())), preferred_element_type=jnp.float32
    )


def gather_rows(shard):
    return lax.all_gather(shard, "tensor", axis=0, tiled=True)


def reduce_rows(left, right, right_dim):
    return lax.psum_scatter(
        contract(left, right, 1, right_dim), "tensor", scatter_dimension=0, tiled=True
    )


def norm_forward(rows, gain, offset):
    center = rows - jnp.mean(rows, axis=1, keepdims=True)
    inverse = lax.rsqrt(jnp.mean(center * center, axis=1, keepdims=True) + EPSILON)
    normed = center * inverse
    return (normed * gain + offset, normed, inverse)


def norm_backward(grad_out, normed, inverse, gain):
    scaled = grad_out * gain
    grad_rows = inverse * (
        scaled
        - jnp.mean(scaled, axis=1, keepdims=True)
        - normed * jnp.mean(scaled * normed, axis=1, keepdims=True)
    )
    return (grad_rows, jnp.sum(grad_out * normed, axis=0), jnp.sum(grad_out, axis=0))


BF = jnp.bfloat16
F32 = jnp.float32


def attend_forward_kernel(rows_ref, weight_ref, bias_ref, down_ref, across_ref, qkv_ref, context_ref):
    width = context_ref.shape[2]
    mixed = jnp.dot(rows_ref[0], weight_ref[...], preferred_element_type=F32) + bias_ref[...]
    low = mixed.astype(BF)
    qkv_ref[0] = low
    same_doc = down_ref[0] == across_ref[0]
    for start in range(0, width, HD):
        queries = low[:, start : start + HD]
        key_rows = low[:, width + start : width + start + HD]
        value_rows = low[:, 2 * width + start : 2 * width + start + HD]
        scores = contract(queries, key_rows, 1, 1) * HD ** (-0.5)
        scores = jnp.where(same_doc, scores, NEGATIVE)
        expos = jnp.exp(scores - jnp.max(scores, axis=1, keepdims=True))
        probs = expos / jnp.sum(expos, axis=1, keepdims=True)
        context = jnp.dot(probs.astype(BF), value_rows, preferred_element_type=F32)
        context_ref[0, :, start : start + HD] = context.astype(BF)


def attend_backward_kernel(
    rows_ref, weight_ref, qkv_ref, grad_ref, down_ref, across_ref, part_ref, weight_grad_ref, bias_grad_ref, mixed_ref
):
    width = grad_ref.shape[2]
    same_doc = down_ref[0] == across_ref[0]
    scale_factor = HD ** (-0.5)
    for start in range(0, width, HD):
        queries = qkv_ref[0, :, start : start + HD]
        key_rows = qkv_ref[0, :, width + start : width + start + HD]
        value_rows = qkv_ref[0, :, 2 * width + start : 2 * width + start + HD]
        grad_context = grad_ref[0, :, start : start + HD]
        scores = contract(key_rows, queries, 1, 1) * scale_factor
        scores = jnp.where(same_doc, scores, NEGATIVE)
        expos = jnp.exp(scores - jnp.max(scores, axis=0, keepdims=True))
        probs = expos / jnp.sum(expos, axis=0, keepdims=True)
        grad_probs = contract(value_rows, grad_context, 1, 1)
        inner = jnp.sum(probs * grad_probs, axis=0, keepdims=True)
        grad_scores = (probs * (grad_probs - inner)).astype(BF)
        mixed_ref[:, start : start + HD] = (contract(grad_scores, key_rows, 0, 0) * scale_factor).astype(BF)
        mixed_ref[:, width + start : width + start + HD] = (
            jnp.dot(grad_scores, queries, preferred_element_type=F32) * scale_factor
        ).astype(BF)
        mixed_ref[:, 2 * width + start : 2 * width + start + HD] = jnp.dot(
            probs.astype(BF), grad_context, preferred_element_type=F32
        ).astype(BF)
    mixed = mixed_ref[...]
    part_ref[0] = contract(mixed, weight_ref[...], 1, 1).astype(part_ref.dtype)
    weight_part = contract(rows_ref[0], mixed, 0, 0)
    bias_part = jnp.sum(mixed.astype(F32), axis=0, keepdims=True)

    @pl.when(pl.program_id(0) == 0)
    def _():
        weight_grad_ref[...] = weight_part
        bias_grad_ref[...] = bias_part

    @pl.when(pl.program_id(0) > 0)
    def _():
        weight_grad_ref[...] += weight_part
        bias_grad_ref[...] += bias_part


def by_sequence(shape):
    return pl.BlockSpec((1,) + shape, lambda item: (item, 0, 0))


def shared_block(shape):
    return pl.BlockSpec(shape, lambda item: (0, 0))


def attend_forward(rows, weight, bias, down_ids, across_ids):
    count, length, model = rows.shape
    triple = weight.shape[1]
    width = triple // 3
    return pl.pallas_call(
        attend_forward_kernel,
        grid=(count,),
        in_specs=[
            by_sequence((length, model)),
            shared_block((model, triple)),
            shared_block((1, triple)),
            by_sequence((length, 1)),
            by_sequence((1, length)),
        ],
        out_specs=[by_sequence((length, triple)), by_sequence((length, width))],
        out_shape=[
            jax.ShapeDtypeStruct((count, length, triple), BF),
            jax.ShapeDtypeStruct((count, length, width), BF),
        ],
        compiler_params=pltpu.CompilerParams(vmem_limit_bytes=48 * 2**20),
        name="attend_forward",
    )(rows, weight, bias, down_ids, across_ids)


def attend_backward(rows, weight, qkv, grad_context, down_ids, across_ids):
    count, length, model = rows.shape
    triple = weight.shape[1]
    width = triple // 3
    return pl.pallas_call(
        attend_backward_kernel,
        grid=(count,),
        in_specs=[
            by_sequence((length, model)),
            shared_block((model, triple)),
            by_sequence((length, triple)),
            by_sequence((length, width)),
            by_sequence((length, 1)),
            by_sequence((1, length)),
        ],
        out_specs=[by_sequence((length, model)), shared_block((model, triple)), shared_block((1, triple))],
        out_shape=[
            jax.ShapeDtypeStruct((count, length, model), BF),
            jax.ShapeDtypeStruct((model, triple), F32),
            jax.ShapeDtypeStruct((1, triple), F32),
        ],
        scratch_shapes=[pltpu.VMEM((length, triple), BF)],
        compiler_params=pltpu.CompilerParams(vmem_limit_bytes=48 * 2**20),
        name="attend_backward",
    )(rows, weight, qkv, grad_context, down_ids, across_ids)


def adam_update(master, moment_one, moment_two, gradient, step_rate, decay_rate):
    one_new = 0.9 * moment_one + 0.1 * gradient
    two_new = 0.999 * moment_two + 0.001 * gradient * gradient
    one_hat = one_new / (1.0 - 0.9**STEP)
    two_hat = two_new / (1.0 - 0.999**STEP)
    updated = master - step_rate * (one_hat / (jnp.sqrt(two_hat) + 1e-08) + decay_rate * master)
    return (updated, one_new, two_new)


def shards(
    inputs,
    cotangent,
    segment_ids,
    qkv_weight,
    qkv_first,
    qkv_second,
    out_weight,
    out_first,
    out_second,
    up_weight,
    up_first,
    up_second,
    down_weight,
    down_first,
    down_second,
    vectors,
    vectors_first,
    vectors_second,
    unit_bias,
    unit_bias_first,
    unit_bias_second,
):
    tensor_rank = lax.axis_index("tensor")
    model = inputs.shape[2]
    head_width = qkv_weight.shape[2]
    unit_width = up_weight.shape[1]
    head_start = tensor_rank * head_width
    unit_start = tensor_rank * unit_width
    triple = 3 * head_width
    unit_slice = lax.dynamic_slice_in_dim(unit_bias, unit_start, unit_width, 0)
    head_slices = lax.dynamic_slice_in_dim(vectors[:2], head_start, head_width, 1)
    qkv_bias = jnp.concatenate([head_slices[0], jnp.zeros((head_width,), F32), head_slices[1]])[None]
    micro_count, local_count, _ = inputs.shape

    def gather(rows):
        return lax.all_gather(rows.astype(BF), "tensor", axis=1, tiled=True)

    def scatter(partial):
        return lax.psum_scatter(partial.astype(BF), "tensor", scatter_dimension=1, tiled=True).astype(F32)

    def flat(rows):
        return rows.reshape(-1, rows.shape[-1])

    def unflat(rows):
        return rows.reshape(micro_count, -1, rows.shape[-1])

    qkv_flat = lax.all_gather(
        qkv_weight.reshape(-1, triple).astype(BF), "fsdp", axis=0, tiled=True
    )
    others = lax.all_gather(
        jnp.concatenate([out_weight.T, up_weight, down_weight.T], axis=1).astype(BF), "fsdp", axis=0, tiled=True
    )
    out_turned = others[:, :head_width]
    up_full = others[:, head_width : head_width + unit_width]
    down_turned = others[:, head_width + unit_width :]

    whole = gather(inputs)
    length = whole.shape[1]
    sequences = whole.reshape(-1, SEQ, model)
    ids = segment_ids.reshape(-1, SEQ)
    down_ids, across_ids = ids[:, :, None], ids[:, None, :]
    qkv_rows, context = attend_forward(sequences, qkv_flat, qkv_bias, down_ids, across_ids)
    context_flat = flat(context)
    branch = scatter(unflat(contract(context_flat, out_turned, 1, 1)))
    residual_one = flat(inputs).astype(F32) + flat(branch) + vectors[2]
    first_norm, normed_one, inverse_one = norm_forward(residual_one, vectors[4], vectors[5])
    first_whole = flat(gather(unflat(first_norm.astype(BF))))
    hidden = jnp.dot(first_whole, up_full, preferred_element_type=F32) + unit_slice
    active_float, gelu_pull = jax.vjp(lambda pre_act: jax.nn.gelu(pre_act, approximate=False), hidden)
    active = active_float.astype(BF)
    second = flat(scatter(unflat(contract(active, down_turned, 1, 1))))
    residual_two = first_norm + second + vectors[3]
    result_rows, normed_two, inverse_two = norm_forward(residual_two, vectors[6], vectors[7])
    layer_output = unflat(result_rows.astype(BF))
    back_rows = flat(cotangent).astype(F32)
    grad_two, gain_two_grad, offset_two_grad = norm_backward(back_rows, normed_two, inverse_two, vectors[6])
    down_bias_grad = jnp.sum(grad_two, axis=0)
    grad_branch_two = flat(gather(unflat(grad_two.astype(BF))))
    grad_active = jnp.dot(grad_branch_two, down_turned, preferred_element_type=F32)
    grad_hidden = gelu_pull(grad_active)[0].astype(BF)
    first_back = scatter(unflat(contract(grad_hidden, up_full, 1, 1)))
    down_grad = contract(grad_branch_two, active, 0, 0)
    up_grad = contract(first_whole, grad_hidden, 0, 0)
    unit_part = jnp.sum(grad_hidden.astype(F32), axis=0)
    wide_total = lax.psum_scatter(
        jnp.concatenate([up_grad, down_grad], axis=1).astype(BF), "fsdp", scatter_dimension=0, tiled=True
    ).astype(F32)
    grad_first = grad_two + flat(first_back)
    grad_one, gain_one_grad, offset_one_grad = norm_backward(grad_first, normed_one, inverse_one, vectors[4])
    out_bias_grad = jnp.sum(grad_one, axis=0)
    grad_branch_one = flat(gather(unflat(grad_one.astype(BF))))
    grad_context = jnp.dot(grad_branch_one, out_turned, preferred_element_type=F32).astype(BF)
    out_grad = contract(grad_branch_one, context_flat, 0, 0)
    input_parts, qkv_grad, qkv_bias_grad = attend_backward(
        sequences, qkv_flat, qkv_rows, grad_context.reshape(context.shape), down_ids, across_ids
    )
    input_grad = unflat(grad_one + flat(scatter(input_parts.reshape(micro_count, length, model))))
    narrow_total = lax.psum_scatter(
        jnp.concatenate([qkv_grad, out_grad], axis=1).astype(BF), "fsdp", scatter_dimension=0, tiled=True
    ).astype(F32)
    zero_rows = jnp.zeros((2, model), F32)
    qv_grad = lax.dynamic_update_slice_in_dim(
        zero_rows, jnp.concatenate([qkv_bias_grad[:, :head_width], qkv_bias_grad[:, 2 * head_width :]], axis=0), head_start, 1
    )
    vector_grad = jnp.concatenate(
        [
            qv_grad,
            jnp.stack(
                [
                    out_bias_grad,
                    down_bias_grad,
                    gain_one_grad,
                    offset_one_grad,
                    gain_two_grad,
                    offset_two_grad,
                ],
                axis=0,
            ),
        ],
        axis=0,
    )
    unit_grad = lax.dynamic_update_slice_in_dim(jnp.zeros(unit_bias.shape, F32), unit_part, unit_start, 0)
    small = lax.psum(jnp.concatenate([vector_grad, unit_grad.reshape(-1, model)], axis=0), ("fsdp", "tensor"))
    grad_totals = (
        narrow_total[:, :triple].reshape(qkv_weight.shape),
        narrow_total[:, triple:].T,
        wide_total[:, :unit_width],
        wide_total[:, unit_width:].T,
    )
    vector_total, unit_total = small[:8], small[8:].reshape(unit_bias.shape)
    masters = (qkv_weight, out_weight, up_weight, down_weight, vectors, unit_bias)
    firsts = (qkv_first, out_first, up_first, down_first, vectors_first, unit_bias_first)
    seconds = (qkv_second, out_second, up_second, down_second, vectors_second, unit_bias_second)
    gradients = (
        grad_totals[0],
        grad_totals[1],
        grad_totals[2],
        grad_totals[3],
        vector_total,
        unit_total,
    )
    news = [
        adam_update(
            masters[place],
            firsts[place],
            seconds[place],
            gradients[place],
            LEARNING_RATES[place],
            WEIGHT_DECAYS[place],
        )
        for place in range(6)
    ]
    return (
        layer_output,
        input_grad,
        news[0][0],
        news[0][1],
        news[0][2],
        news[1][0],
        news[1][1],
        news[1][2],
        news[2][0],
        news[2][1],
        news[2][2],
        news[3][0],
        news[3][1],
        news[3][2],
        news[4][0],
        news[4][1],
        news[4][2],
        news[5][0],
        news[5][1],
        news[5][2],
    )


def solution(mesh):
    placed = (
        P(None, ("fsdp", "tensor"), None),
        P(None, ("fsdp", "tensor"), None),
        P(None, "fsdp"),
        P("fsdp", None, "tensor"),
        P("fsdp", None, "tensor"),
        P("fsdp", None, "tensor"),
        P("tensor", "fsdp"),
        P("tensor", "fsdp"),
        P("tensor", "fsdp"),
        P("fsdp", "tensor"),
        P("fsdp", "tensor"),
        P("fsdp", "tensor"),
        P("tensor", "fsdp"),
        P("tensor", "fsdp"),
        P("tensor", "fsdp"),
        P(),
        P(),
        P(),
        P(),
        P(),
        P(),
    )
    return jax.shard_map(
        shards,
        mesh=mesh,
        in_specs=placed,
        out_specs=(
            P(None, ("fsdp", "tensor"), None),
            P(None, ("fsdp", "tensor"), None),
            P("fsdp", None, "tensor"),
            P("fsdp", None, "tensor"),
            P("fsdp", None, "tensor"),
            P("tensor", "fsdp"),
            P("tensor", "fsdp"),
            P("tensor", "fsdp"),
            P("fsdp", "tensor"),
            P("fsdp", "tensor"),
            P("fsdp", "tensor"),
            P("tensor", "fsdp"),
            P("tensor", "fsdp"),
            P("tensor", "fsdp"),
            P(),
            P(),
            P(),
            P(),
            P(),
            P(),
        ),
        check_vma=False,
    )
```

time: 654 us -> 471 us (0.72); the launches traced: 643 us -> 467 us
  blocking collectives: 206 us -> 50.3 us
  waiting for transfers between devices: 252 us -> 294 us
  matrix products: 82 us -> 40.4 us
  local copies, waits for them, and re-layouts: 45.5 us -> 19.8 us
  Pallas kernels: 0 us -> 18 us
  other arithmetic: 39.2 us -> 29.3 us
    all_gather x10 -> x1, blocking collectives: 161 us -> 11.3 us  [shards(): lax.all_gather(qkv_weight.reshape(-1, triple).astype(BF), 'fsdp', axis=0,...]
    all_gather x2 -> x5, waiting for transfers between devices: 0.01 us -> 148 us  [the longest x4 121 us: gather(): return lax.all_gather(rows.astype(BF), 'tensor', axis=1, tiled=True)]
    reduce_scatter x11 -> x6, waiting for transfers between devices: 252 us -> 144 us  [the longest x4 125 us: scatter(): lax.psum_scatter(partial.astype(BF), 'tensor', scatter_dimension=1, tiled...]
    dot_general x50 -> x6, matrix products: 58.8 us -> 19.7 us  [contract(): lax.dot_general(left, right, (((left_dim,), (right_dim,)), ((), ())), pre...]
    pallas_call x0 -> x2, Pallas kernels: none -> 18 us  [the longest x1 13 us: attend_backward(): pl.pallas_call(attend_backward_kernel, grid=(count,), in_specs=[by_sequen...]
    dynamic_slice x19 -> x0, local copies, waits for them, and re-layouts: 9.08 us -> none  [the longest x12 4.29 us: shards(): lax.map(attend_forward, (query_items, key_items, value_items, segment_ite...]
    dot_general x16 -> x3, matrix products: 23.2 us -> 20.7 us  [the longest x1 11.6 us: shards(): jnp.dot(first_whole, up_full, preferred_element_type=F32) + unit_slice]
    unnamed x181 -> x69, local copies, waits for them, and re-layouts: 11 us -> 13.2 us
  transfers between devices with their start and end apart: 14 -> 11, of which waited for: 9 -> 10; matrix products, arithmetic and copies ran while one was open for 18% -> 9% of each run, Pallas kernels for 0% -> 4%
where the time goes in v1:
time: 471 us; the launch traced here: 467 us
  waiting for transfers between devices  294 us (62%)
  blocking collectives  50.3 us (11%)
  matrix products  40.4 us (9%)
  other arithmetic  29.3 us (6%)
  local copies, waits for them, and re-layouts  19.8 us (4%)
  Pallas kernels  18 us (4%)
  between operations  14.5 us (3%)
    reduce_scatter x4, waiting for transfers between devices, scatter(): lax.psum_scatter(partial.astype(BF), 'tensor', scatter_dimension=1, tiled...  125 us
    all_gather x4, waiting for transfers between devices, gather(): return lax.all_gather(rows.astype(BF), 'tensor', axis=1, tiled=True)  121 us
    psum x1, blocking collectives, shards(): lax.psum(jnp.concatenate([vector_grad, unit_grad.reshape(-1, model)], axi...  38.9 us
    all_gather x1, waiting for transfers between devices, shards(): lax.all_gather(jnp.concatenate([out_weight.T, up_weight, down_weight.T],...  27.3 us
    dot_general x6, matrix products, contract(): lax.dot_general(left, right, (((left_dim,), (right_dim,)), ((), ())), pre...  19.7 us
    reduce_scatter x1, waiting for transfers between devices, shards(): lax.psum_scatter(jnp.concatenate([up_grad, down_grad], axis=1).astype(BF)...  19.4 us
    unnamed x69, local copies, waits for them, and re-layouts  13.2 us
    pallas_call x1, Pallas kernels, attend_backward(): pl.pallas_call(attend_backward_kernel, grid=(count,), in_specs=[by_sequen...  13 us
  transfers between devices with their start and end apart: 11, of which 10 were waited for; matrix products, arithmetic and copies ran while one was open for 9% of the time, Pallas kernels for 4%

profile of v1, /device:TPU:9, one launch (start us, length us, event | category | flops | bytes accessed | tf_op | source)
XLA Modules:
  0.0 466.8 jit_solution(2226720009403340280)
XLA Ops:
  13.8 11.3 %all_gather.19.weight_ref = bf16[768,576]{1,0:T(8,128)(2,1)S(1)} all-gather(bf16[96,576]{1,0:T(8,128)(2,1)S(1)} %copy.151), channel_id=1, replica_groups=mesh['fsdp'=8,'tensor'=4] {'fsdp'}, dimensions={0}, use_global_device_ids=true | all-gather | bytes 995328 | tf_op jit(solution)/shard_map/all_gather | solution.py:231
  25.1 21.6 %all-gather.6.cloned.1.call-done.rows_ref = bf16[2,512,768]{2,1,0:T(8,128)(2,1)} async-done(((bf16[2,128,768]{2,1,0:T(8,128)(2,1)}), bf16[2,512,768]{2,1,0:T(8,128)(2,1)}) %all-gather.6.cloned.1.call-update) | async-done | bytes 1572880 | tf_op jit(solution)/shard_map/all_gather | solution.py:220
  48.1 4.9 %attend_forward.1 = (bf16[2,512,576]{2,1,0:T(8,128)(2,1)S(1)}, bf16[2,512,192]{2,1,0:T(8,128)(2,1)S(1)}) custom-call(bf16[2,512,768]{2,1,0:T(8,128)(2,1)S(1)} %copy-done, bf16[768,576]{1,0:T(8,128)(2,1)S(1)} %all_gather.19.weight_ref, f32[1,576]{1,0:T(1,128)S(1)} %broadcast_in_dim.11.bias_ref, s32[2,512,1]{2,1,0:T(8,128)S(1)} %copy.152.down_ref, ...), custom_call_target="tpu_custom_call" | custom-call | tf_op jit(solution)/shard_map/attend_forward/pallas_call | solution.py:128
  53.0 27.3 %all-gather.8.cloned.1.call-done = bf16[768,1728]{1,0:T(8,128)(2,1)} async-done(((bf16[96,1728]{1,0:T(8,128)(2,1)}), bf16[768,1728]{1,0:T(8,128)(2,1)}) %all-gather.8.cloned.1.call-update) | async-done | bytes 2654224 | tf_op jit(solution)/shard_map/all_gather | solution.py:234
  80.4 2.8 convolution_convert_fusion.2
  83.3 33.0 %reduce-scatter.9.cloned.1.call-done = bf16[2,128,768]{2,1,0:T(8,128)(2,1)} async-done(((bf16[2,512,768]{2,1,0:T(8,128)(2,1)}), bf16[2,128,768]{2,1,0:T(8,128)(2,1)}) %reduce-scatter.9.cloned.1.call-update) | async-done | bytes 393232 | tf_op jit(solution)/shard_map/reduce_scatter | solution.py:223
  119.0 2.1 fusion.22
  121.3 36.7 %all-gather.10.cloned.1.call-done = bf16[2,512,768]{2,1,0:T(8,128)(2,1)} async-done(((bf16[2,128,768]{2,1,0:T(8,128)(2,1)}), bf16[2,512,768]{2,1,0:T(8,128)(2,1)}) %all-gather.10.cloned.1.call-update) | async-done | bytes 1572880 | tf_op jit(solution)/shard_map/all_gather | solution.py:220
  158.0 11.6 %multiply_convert_fusion = (bf16[1024,768]{1,0:T(8,128)(2,1)S(1)}, f32[1024,768]{1,0:T(8,128)}, f32[1024,768]{1,0:T(8,128)}) fusion(f32[768]{0:T(1024)S(1)} %dynamic_slice.7, bf16[1024,768]{1,0:T(8,128)(2,1)} %bitcast.61, bf16[768,1728]{1,0:T(8,128)(2,1)} %all-gather.8.cloned.1.call-done), kind=kOutput, calls=%fused_computation.4 | convolution fusion | flops 1259864064 | bytes 10619904 | tf_op jit(solution)/shard_map/dot_general | solution.py:252
  169.7 4.6 convolution_convert_fusion.1
  174.5 33.4 %reduce-scatter.11.cloned.1.call-done = bf16[2,128,768]{2,1,0:T(8,128)(2,1)} async-done(((bf16[2,512,768]{2,1,0:T(8,128)(2,1)}), bf16[2,128,768]{2,1,0:T(8,128)(2,1)}) %reduce-scatter.11.cloned.1.call-update) | async-done | bytes 393232 | tf_op jit(solution)/shard_map/reduce_scatter | solution.py:223
  208.0 1.6 fusion.43
  212.8 36.8 %all-gather.12.cloned.1.call-done = bf16[2,512,768]{2,1,0:T(8,128)(2,1)} async-done(((bf16[2,128,768]{2,1,0:T(8,128)(2,1)}), bf16[2,512,768]{2,1,0:T(8,128)(2,1)}) %all-gather.12.cloned.1.call-update) | async-done | bytes 1572880 | tf_op jit(solution)/shard_map/all_gather | solution.py:220
  249.6 6.2 %convert_reduce_fusion = (f32[768]{0:T(1024)S(1)}, bf16[1024,768]{1,0:T(8,128)(2,1)S(1)}) fusion(f32[1024,768]{1,0:T(8,128)} %get-tuple-element.150, bf16[1024,768]{1,0:T(8,128)(2,1)} %bitcast.63, bf16[768,1728]{1,0:T(8,128)(2,1)} %all-gather.8.cloned.1.call-done, f32[1024,768]{1,0:T(8,128)} %get-tuple-element.156, f32[768]{0:T(1024)S(1)} %dynamic_slice.7), kind=kOutput, calls=%fused_computation.2 | convolution fusion | flops 1221328128 | bytes 10622976 | tf_op jit(solution)/shard_map/dot_general | solution.py:263
  255.8 4.6 convolution_convert_fusion
  260.5 33.6 %reduce-scatter.13.cloned.1.call-done = bf16[2,128,768]{2,1,0:T(8,128)(2,1)} async-done(((bf16[2,512,768]{2,1,0:T(8,128)(2,1)}), bf16[2,128,768]{2,1,0:T(8,128)(2,1)}) %reduce-scatter.13.cloned.1.call-update) | async-done | bytes 393232 | tf_op jit(solution)/shard_map/reduce_scatter | solution.py:223
  294.1 1.9 multiply_reduce_fusion
  296.0 1.8 fusion.36
  299.5 3.5 convolution_convert_fusion.3
  304.5 1.5 pad_maximum_fusion
  306.1 4.3 copy.178
  310.7 25.7 %all-gather.14.cloned.1.call-done = bf16[2,512,768]{2,1,0:T(8,128)(2,1)} async-done(((bf16[2,128,768]{2,1,0:T(8,128)(2,1)}), bf16[2,512,768]{2,1,0:T(8,128)(2,1)}) %all-gather.14.cloned.1.call-update) | async-done | bytes 1572880 | tf_op jit(solution)/shard_map/all_gather | solution.py:220
  336.3 2.9 convolution_convert_fusion.5
  340.4 2.7 fusion.6
  343.2 1.9 copy.160
  345.1 13.0 %attend_backward.1 = (bf16[2,512,768]{2,1,0:T(8,128)(2,1)}, f32[768,576]{1,0:T(8,128)}, f32[1,576]{1,0:T(1,128)S(1)}) custom-call(bf16[2,512,768]{2,1,0:T(8,128)(2,1)} %all-gather.6.cloned.1.call-done.rows_ref, bf16[768,576]{1,0:T(8,128)(2,1)S(1)} %all_gather.19.weight_ref, bf16[2,512,576]{2,1,0:T(8,128)(2,1)S(1)} %get-tuple-element.26.qkv_ref, ...), custom_call_target="tpu_custom_call" | custom-call | tf_op jit(solution)/shard_map/attend_backward/pallas_call | solution.py:152
  358.1 1.6 convert.26
  362.9 19.4 %reduce-scatter.19.cloned.1.call-done = bf16[96,1536]{1,0:T(8,128)(2,1)} async-done(((bf16[768,1536]{1,0:T(8,128)(2,1)}), bf16[96,1536]{1,0:T(8,128)(2,1)}) %reduce-scatter.19.cloned.1.call-update) | async-done | bytes 294928 | tf_op jit(solution)/shard_map/reduce_scatter | solution.py:269
  384.4 2.1 multiply_subtract_fusion
  386.9 38.9 %psum.7 = f32[12,768]{1,0:T(8,128)S(1)} all-reduce(f32[12,768]{1,0:T(8,128)S(1)} %concatenate.26), channel_id=1, replica_groups=mesh['fsdp'=8,'tensor'=4] {'fsdp','tensor'}, use_global_device_ids=true, to_apply=%region_21.0 | all-reduce | flops 9216 | bytes 73728 | tf_op jit(solution)/shard_map/psum | solution.py:307
  433.6 24.7 %reduce-scatter.15.cloned.1.call-done = bf16[2,128,768]{2,1,0:T(8,128)(2,1)} async-done(((bf16[2,512,768]{2,1,0:T(8,128)(2,1)}), bf16[2,128,768]{2,1,0:T(8,128)(2,1)}) %reduce-scatter.15.cloned.1.call-update) | async-done | bytes 393232 | tf_op jit(solution)/shard_map/reduce_scatter | solution.py:223
  458.3 2.0 convert_add_fusion
  (149 shorter events, 32.2 us)
Async XLA Ops:
  7.2 6.1 %slice-start = ((f32[8,768]{1,0:T(8,128)}), f32[2,768]{1,0:T(2,128)S(1)}, s32[]{:S(2)}) async-start(f32[8,768]{1,0:T(8,128)} %param.36), calls=%async_computation.17 | async-start | bytes 12288 | tf_op jit(solution)/shard_map/slice | solution.py:215
  7.2 6.3 %copy-start.21 = (s32[2,512]{1,0:T(2,128)S(1)}, s32[2,512]{1,0:T(2,128)}, u32[]{:S(2)}) copy-start(s32[2,512]{1,0:T(2,128)} %param.23) | copy-start | bytes 12292
  7.2 39.5 %all-gather.6.cloned.1.call-start = ((), (), s32[]{:S(2)}) async-start(), calls=%async_computation.6 | async-start | bytes 1966080 | tf_op jit(solution)/shard_map/all_gather | solution.py:220
  7.9 72.4 %all-gather.8.cloned.1.call-start = ((), (), s32[]{:S(2)}) async-start(), calls=%async_computation.7 | async-start | bytes 3096576 | tf_op jit(solution)/shard_map/all_gather | solution.py:234
  12.0 104.3 %reduce-scatter.9.cloned.1.call-start = ((), (), s32[]{:S(2)}) async-start(), calls=%async_computation.8 | async-start | bytes 1966080 | tf_op jit(solution)/shard_map/reduce_scatter | solution.py:223
  48.1 35.1 %copy-start.17 = (f32[8,768]{1,0:T(8,128)S(1)}, f32[8,768]{1,0:T(8,128)}, u32[]{:S(2)}) copy-start(f32[8,768]{1,0:T(8,128)} %param.36) | copy-start | bytes 73732
  53.0 68.1 %copy-start.1 = (bf16[2,512,192]{2,1,0:T(8,128)(2,1)}, bf16[2,512,192]{2,1,0:T(8,128)(2,1)S(1)}, u32[]{:S(2)}) copy-start(bf16[2,512,192]{2,1,0:T(8,128)(2,1)S(1)} %get-tuple-element.25) | copy-start | bytes 1179652
  80.3 40.9 %copy-start.20 = (f32[3072]{0:T(1024)S(1)}, f32[3072]{0:T(1024)}, u32[]{:S(2)}) copy-start(f32[3072]{0:T(1024)} %param.39) | copy-start | bytes 36868
  83.2 74.9 %all-gather.10.cloned.1.call-start = ((), (), s32[]{:S(2)}) async-start(), calls=%async_computation.9 | async-start | bytes 1966080 | tf_op jit(solution)/shard_map/all_gather | solution.py:220
  121.2 86.8 %reduce-scatter.11.cloned.1.call-start = ((), (), s32[]{:S(2)}) async-start(), calls=%async_computation.10 | async-start | bytes 1966080 | tf_op jit(solution)/shard_map/reduce_scatter | solution.py:223
  169.7 4.6 copy-start.25
  169.7 38.3 %copy-start.2 = (bf16[2,128,768]{2,1,0:T(8,128)(2,1)S(1)}, bf16[2,128,768]{2,1,0:T(8,128)(2,1)}, u32[]{:S(2)}) copy-start(bf16[2,128,768]{2,1,0:T(8,128)(2,1)} %param.21) | copy-start | bytes 1179652
  174.3 75.3 %all-gather.12.cloned.1.call-start = ((), (), s32[]{:S(2)}) async-start(), calls=%async_computation.11 | async-start | bytes 1966080 | tf_op jit(solution)/shard_map/all_gather | solution.py:220
  212.8 81.3 %reduce-scatter.13.cloned.1.call-start = ((), (), s32[]{:S(2)}) async-start(), calls=%async_computation.12 | async-start | bytes 1966080 | tf_op jit(solution)/shard_map/reduce_scatter | solution.py:223
  255.8 4.6 copy-start.26
  260.4 75.9 %all-gather.14.cloned.1.call-start = ((), (), s32[]{:S(2)}) async-start(), calls=%async_computation.13 | async-start | bytes 1966080 | tf_op jit(solution)/shard_map/all_gather | solution.py:220
  299.5 82.8 %reduce-scatter.19.cloned.1.call-start = ((), (), s32[]{:S(2)}) async-start(), calls=%async_computation.16 | async-start | bytes 2654208 | tf_op jit(solution)/shard_map/reduce_scatter | solution.py:269
  299.5 3.5 copy-start.24
  299.5 3.5 copy-start.27
  310.4 116.7 %reduce-scatter.17.cloned.1.call-start = ((), (), s32[]{:S(2)}) async-start(), calls=%async_computation.15 | async-start | bytes 1327104 | tf_op jit(solution)/shard_map/reduce_scatter | solution.py:282
  345.0 14.7 %copy-start.5 = (bf16[768,192]{1,0:T(8,128)(2,1)S(1)}, bf16[768,192]{1,0:T(8,128)(2,1)}, u32[]{:S(2)}) copy-start(bf16[768,192]{1,0:T(8,128)(2,1)} %copy.160) | copy-start | bytes 884740
  361.0 22.3 %copy-start.8 = (f32[96,768]{1,0:T(8,128)S(1)}, f32[96,768]{1,0:T(8,128)}, u32[]{:S(2)}) copy-start(f32[96,768]{1,0:T(8,128)} %param.30) | copy-start | bytes 884740
  361.0 22.3 %copy-start.13 = (f32[96,768]{1,0:T(8,128)S(1)}, f32[96,768]{1,0:T(8,128)}, u32[]{:S(2)}) copy-start(f32[96,768]{1,0:T(8,128)} %param.31) | copy-start | bytes 884740
  361.0 22.3 %copy-start.14 = (f32[96,768]{1,0:T(8,128)S(1)}, f32[96,768]{1,0:T(8,128)}, u32[]{:S(2)}) copy-start(f32[96,768]{1,0:T(8,128)} %param.32) | copy-start | bytes 884740
  361.1 97.2 %reduce-scatter.15.cloned.1.call-start = ((), (), s32[]{:S(2)}) async-start(), calls=%async_computation.14 | async-start | bytes 1966080 | tf_op jit(solution)/shard_map/reduce_scatter | solution.py:223
  361.1 23.3 %copy-start.9 = (f32[768,96]{0,1:T(8,128)S(1)}, f32[768,96]{0,1:T(8,128)}, u32[]{:S(2)}) copy-start(f32[768,96]{0,1:T(8,128)} %param.33) | copy-start | bytes 884740
  362.1 63.7 %copy-start.22 = (f32[3072]{0:T(1024)S(1)}, f32[3072]{0:T(1024)}, u32[]{:S(2)}) copy-start(f32[3072]{0:T(1024)} %param.40) | copy-start | bytes 36868
  362.1 63.7 %copy-start.23 = (f32[3072]{0:T(1024)S(1)}, f32[3072]{0:T(1024)}, u32[]{:S(2)}) copy-start(f32[3072]{0:T(1024)} %param.41) | copy-start | bytes 36868
  362.2 64.3 %copy-start.18 = (f32[8,768]{1,0:T(8,128)S(1)}, f32[8,768]{1,0:T(8,128)}, u32[]{:S(2)}) copy-start(f32[8,768]{1,0:T(8,128)} %param.37) | copy-start | bytes 73732
  362.2 64.3 %copy-start.19 = (f32[8,768]{1,0:T(8,128)S(1)}, f32[8,768]{1,0:T(8,128)}, u32[]{:S(2)}) copy-start(f32[8,768]{1,0:T(8,128)} %param.38) | copy-start | bytes 73732
  427.1 4.0 copy-start.10
  428.1 30.1 %copy-start.4 = (f32[2,128,768]{2,1,0:T(8,128)S(1)}, f32[2,128,768]{2,1,0:T(8,128)}, u32[]{:S(2)}) copy-start(f32[2,128,768]{2,1,0:T(8,128)} %copy-done.3) | copy-start | bytes 2359300
  (8 other events, 17.4 us)
Sparse Core Ops, SparseCore 0:
  9.6 37.0 all-gather.5
  49.1 31.1 all-gather.7
  83.3 32.9 reduce-scatter.8
  121.3 36.6 all-gather.9
  174.4 33.5 reduce-scatter.10
  212.9 36.6 all-gather.11
  260.5 33.4 reduce-scatter.12
  299.6 36.7 all-gather.13
  339.7 42.5 reduce-scatter.18
  385.7 36.7 reduce-scatter.16
  424.8 33.4 reduce-scatter.14

commit v2 on v1

--- a/solution.py
+++ b/solution.py
@@ -3,6 +3,7 @@
 from jax import lax
 from jax.experimental import pallas as pl
 from jax.experimental.pallas import tpu as pltpu
+from jax.sharding import Mesh
 from jax.sharding import PartitionSpec as P
 
 HD = 64
@@ -50,6 +51,7 @@
     return (grad_rows, jnp.sum(grad_out * normed, axis=0), jnp.sum(grad_out, axis=0))
 
 
+FSDP = ("chip", "core")
 BF = jnp.bfloat16
 F32 = jnp.float32
 
@@ -209,18 +211,70 @@
     head_width = qkv_weight.shape[2]
     unit_width = up_weight.shape[1]
     head_start = tensor_rank * head_width
-    unit_start = tensor_rank * unit_width
     triple = 3 * head_width
-    unit_slice = lax.dynamic_slice_in_dim(unit_bias, unit_start, unit_width, 0)
+    chip_count = lax.axis_size("chip")
+    tensor_count = lax.axis_size("tensor")
+    core_rank = lax.axis_index("core")
+    half_width = unit_width // 2
+    depth = up_weight.shape[0]
+    unit_slice = lax.dynamic_index_in_dim(
+        unit_bias.reshape(tensor_count, 2, half_width), core_rank, 1, keepdims=False
+    ).reshape(-1)
     head_slices = lax.dynamic_slice_in_dim(vectors[:2], head_start, head_width, 1)
     qkv_bias = jnp.concatenate([head_slices[0], jnp.zeros((head_width,), F32), head_slices[1]])[None]
     micro_count, local_count, _ = inputs.shape
 
+    def shifted(rows, step):
+        pairs = [(place, (place + step) % tensor_count) for place in range(tensor_count)]
+        return lax.ppermute(rows, "tensor", pairs)
+
     def gather(rows):
-        return lax.all_gather(rows.astype(BF), "tensor", axis=1, tiled=True)
+        rows = rows.astype(BF)
+        whole_rows = jnp.zeros((rows.shape[0], tensor_count) + rows.shape[1:], BF)
+        for step in range(tensor_count):
+            part = shifted(rows, step) if step else rows
+            source = lax.rem(tensor_rank + tensor_count - step, tensor_count)
+            whole_rows = lax.dynamic_update_slice_in_dim(whole_rows, part[:, None], source, 1)
+        return whole_rows.reshape(rows.shape[0], -1, rows.shape[2])
 
     def scatter(partial):
-        return lax.psum_scatter(partial.astype(BF), "tensor", scatter_dimension=1, tiled=True).astype(F32)
+        parts = partial.astype(BF).reshape(partial.shape[0], tensor_count, -1, partial.shape[2])
+        total = lax.dynamic_index_in_dim(parts, tensor_rank, 1, keepdims=False).astype(F32)
+        for step in range(1, tensor_count):
+            target = lax.rem(tensor_rank + step, tensor_count)
+            block = lax.dynamic_index_in_dim(parts, target, 1, keepdims=False)
+            total = total + shifted(block, step).astype(F32)
+        return total
+
+    def swap(rows):
+        return lax.ppermute(rows.astype(BF), "core", [(0, 1), (1, 0)])
+
+    def both(rows):
+        return jnp.concatenate([rows, swap(rows)], axis=0)
+
+    def join(partial):
+        count = partial.shape[0] // 2
+        return partial[:count] + swap(partial[count:]).astype(F32)
+
+    def by_core(mine, other, axis):
+        first_part = jnp.where(core_rank == 0, mine, other)
+        second_part = jnp.where(core_rank == 0, other, mine)
+        return jnp.concatenate([first_part, second_part], axis=axis)
+
+    def sum_everywhere(rows):
+        for name in ("core", "chip", "tensor"):
+            size = lax.axis_size(name)
+            if size & (size - 1):
+                rows = lax.psum(rows, name)
+                continue
+            step = 1
+            while step < size:
+                rows = rows + lax.ppermute(rows, name, [(place, place ^ step) for place in range(size)])
+                step *= 2
+        return rows
+
+    def half(halves, rank, axis):
+        return lax.dynamic_index_in_dim(halves, rank, axis, keepdims=False)
 
     def flat(rows):
         return rows.reshape(-1, rows.shape[-1])
@@ -228,17 +282,27 @@
     def unflat(rows):
         return rows.reshape(micro_count, -1, rows.shape[-1])
 
-    qkv_flat = lax.all_gather(
-        qkv_weight.reshape(-1, triple).astype(BF), "fsdp", axis=0, tiled=True
-    )
-    others = lax.all_gather(
-        jnp.concatenate([out_weight.T, up_weight, down_weight.T], axis=1).astype(BF), "fsdp", axis=0, tiled=True
-    )
-    out_turned = others[:, :head_width]
-    up_full = others[:, head_width : head_width + unit_width]
-    down_turned = others[:, head_width + unit_width :]
-
     whole = gather(inputs)
+    narrow = lax.all_gather(
+        jnp.concatenate([qkv_weight.reshape(-1, triple), out_weight.T], axis=1).astype(BF), FSDP, axis=0, tiled=True
+    )
+    qkv_flat = narrow[:, :triple]
+    out_turned = narrow[:, triple:]
+    wide_shard = jnp.stack([up_weight, down_weight.T], axis=1).astype(BF).reshape(depth, 2, 2, half_width)
+    wide_mine = half(wide_shard, core_rank, 2)
+    wide_other = swap(half(wide_shard, 1 - core_rank, 2))
+    wide_block = by_core(wide_mine, wide_other, 0).reshape(2 * depth, 2 * half_width)
+    wide_full = lax.all_gather(lax.all_gather(wide_block, "tensor"), "chip")
+    up_full, down_turned = (
+        jnp.concatenate(
+            [
+                wide_full[:, place, :, start : start + half_width].reshape(model, half_width)
+                for place in range(tensor_count)
+            ],
+            axis=1,
+        )
+        for start in (0, half_width)
+    )
     length = whole.shape[1]
     sequences = whole.reshape(-1, SEQ, model)
     ids = segment_ids.reshape(-1, SEQ)
@@ -248,28 +312,39 @@
     branch = scatter(unflat(contract(context_flat, out_turned, 1, 1)))
     residual_one = flat(inputs).astype(F32) + flat(branch) + vectors[2]
     first_norm, normed_one, inverse_one = norm_forward(residual_one, vectors[4], vectors[5])
-    first_whole = flat(gather(unflat(first_norm.astype(BF))))
+    first_whole = both(first_norm.astype(BF))
     hidden = jnp.dot(first_whole, up_full, preferred_element_type=F32) + unit_slice
     active_float, gelu_pull = jax.vjp(lambda pre_act: jax.nn.gelu(pre_act, approximate=False), hidden)
     active = active_float.astype(BF)
-    second = flat(scatter(unflat(contract(active, down_turned, 1, 1))))
+    second = join(contract(active, down_turned, 1, 1))
     residual_two = first_norm + second + vectors[3]
     result_rows, normed_two, inverse_two = norm_forward(residual_two, vectors[6], vectors[7])
     layer_output = unflat(result_rows.astype(BF))
     back_rows = flat(cotangent).astype(F32)
     grad_two, gain_two_grad, offset_two_grad = norm_backward(back_rows, normed_two, inverse_two, vectors[6])
     down_bias_grad = jnp.sum(grad_two, axis=0)
-    grad_branch_two = flat(gather(unflat(grad_two.astype(BF))))
+    grad_branch_two = both(grad_two.astype(BF))
     grad_active = jnp.dot(grad_branch_two, down_turned, preferred_element_type=F32)
     grad_hidden = gelu_pull(grad_active)[0].astype(BF)
-    first_back = scatter(unflat(contract(grad_hidden, up_full, 1, 1)))
+    first_back = join(contract(grad_hidden, up_full, 1, 1))
     down_grad = contract(grad_branch_two, active, 0, 0)
     up_grad = contract(first_whole, grad_hidden, 0, 0)
     unit_part = jnp.sum(grad_hidden.astype(F32), axis=0)
-    wide_total = lax.psum_scatter(
-        jnp.concatenate([up_grad, down_grad], axis=1).astype(BF), "fsdp", scatter_dimension=0, tiled=True
-    ).astype(F32)
-    grad_first = grad_two + flat(first_back)
+    up_low, down_low = up_grad.astype(BF), down_grad.astype(BF)
+    wide_grad = jnp.concatenate(
+        [
+            jnp.concatenate(
+                [low[:, start : start + half_width] for low in (up_low, down_low)], axis=1
+            ).reshape(chip_count, 2 * depth, 2 * half_width)
+            for start in range(0, tensor_count * half_width, half_width)
+        ],
+        axis=1,
+    )
+    wide_part = lax.psum_scatter(wide_grad, "chip", scatter_dimension=0, tiled=False)
+    wide_part = lax.psum_scatter(wide_part, "tensor", scatter_dimension=0, tiled=True)
+    wide_part = wide_part.reshape(2, depth, 2, half_width)
+    wide_total = by_core(half(wide_part, core_rank, 0), swap(half(wide_part, 1 - core_rank, 0)), 2).astype(F32)
+    grad_first = grad_two + first_back
     grad_one, gain_one_grad, offset_one_grad = norm_backward(grad_first, normed_one, inverse_one, vectors[4])
     out_bias_grad = jnp.sum(grad_one, axis=0)
     grad_branch_one = flat(gather(unflat(grad_one.astype(BF))))
@@ -280,7 +355,7 @@
     )
     input_grad = unflat(grad_one + flat(scatter(input_parts.reshape(micro_count, length, model))))
     narrow_total = lax.psum_scatter(
-        jnp.concatenate([qkv_grad, out_grad], axis=1).astype(BF), "fsdp", scatter_dimension=0, tiled=True
+        jnp.concatenate([qkv_grad, out_grad], axis=1).astype(BF), FSDP, scatter_dimension=0, tiled=True
     ).astype(F32)
     zero_rows = jnp.zeros((2, model), F32)
     qv_grad = lax.dynamic_update_slice_in_dim(
@@ -303,13 +378,15 @@
         ],
         axis=0,
     )
-    unit_grad = lax.dynamic_update_slice_in_dim(jnp.zeros(unit_bias.shape, F32), unit_part, unit_start, 0)
-    small = lax.psum(jnp.concatenate([vector_grad, unit_grad.reshape(-1, model)], axis=0), ("fsdp", "tensor"))
+    unit_grad = lax.dynamic_update_slice_in_dim(
+        jnp.zeros((tensor_count, 2, half_width), F32), unit_part.reshape(tensor_count, 1, half_width), core_rank, 1
+    )
+    small = sum_everywhere(jnp.concatenate([vector_grad, unit_grad.reshape(-1, model)], axis=0))
     grad_totals = (
         narrow_total[:, :triple].reshape(qkv_weight.shape),
         narrow_total[:, triple:].T,
-        wide_total[:, :unit_width],
-        wide_total[:, unit_width:].T,
+        wide_total[:, 0],
+        wide_total[:, 1].T,
     )
     vector_total, unit_total = small[:8], small[8:].reshape(unit_bias.shape)
     masters = (qkv_weight, out_weight, up_weight, down_weight, vectors, unit_bias)
@@ -360,21 +437,21 @@
 
 def solution(mesh):
     placed = (
-        P(None, ("fsdp", "tensor"), None),
-        P(None, ("fsdp", "tensor"), None),
-        P(None, "fsdp"),
-        P("fsdp", None, "tensor"),
-        P("fsdp", None, "tensor"),
-        P("fsdp", None, "tensor"),
-        P("tensor", "fsdp"),
-        P("tensor", "fsdp"),
-        P("tensor", "fsdp"),
-        P("fsdp", "tensor"),
-        P("fsdp", "tensor"),
-        P("fsdp", "tensor"),
-        P("tensor", "fsdp"),
-        P("tensor", "fsdp"),
-        P("tensor", "fsdp"),
+        P(None, FSDP + ("tensor",), None),
+        P(None, FSDP + ("tensor",), None),
+        P(None, FSDP),
+        P(FSDP, None, "tensor"),
+        P(FSDP, None, "tensor"),
+        P(FSDP, None, "tensor"),
+        P("tensor", FSDP),
+        P("tensor", FSDP),
+        P("tensor", FSDP),
+        P(FSDP, "tensor"),
+        P(FSDP, "tensor"),
+        P(FSDP, "tensor"),
+        P("tensor", FSDP),
+        P("tensor", FSDP),
+        P("tensor", FSDP),
         P(),
         P(),
         P(),
@@ -384,23 +461,23 @@
     )
     return jax.shard_map(
         shards,
-        mesh=mesh,
+        mesh=Mesh(mesh.devices.reshape(-1, 2, mesh.shape["tensor"]), ("chip", "core", "tensor")),
         in_specs=placed,
         out_specs=(
-            P(None, ("fsdp", "tensor"), None),
-            P(None, ("fsdp", "tensor"), None),
-            P("fsdp", None, "tensor"),
-            P("fsdp", None, "tensor"),
-            P("fsdp", None, "tensor"),
-            P("tensor", "fsdp"),
-            P("tensor", "fsdp"),
-            P("tensor", "fsdp"),
-            P("fsdp", "tensor"),
-            P("fsdp", "tensor"),
-            P("fsdp", "tensor"),
-            P("tensor", "fsdp"),
-            P("tensor", "fsdp"),
-            P("tensor", "fsdp"),
+            P(None, FSDP + ("tensor",), None),
+            P(None, FSDP + ("tensor",), None),
+            P(FSDP, None, "tensor"),
+            P(FSDP, None, "tensor"),
+            P(FSDP, None, "tensor"),
+            P("tensor", FSDP),
+            P("tensor", FSDP),
+            P("tensor", FSDP),
+            P(FSDP, "tensor"),
+            P(FSDP, "tensor"),
+            P(FSDP, "tensor"),
+            P("tensor", FSDP),
+            P("tensor", FSDP),
+            P("tensor", FSDP),
             P(),
             P(),
             P(),

time: 471 us -> 321 us (0.68)
  waiting for transfers between devices: 294 us -> 188 us
  blocking collectives: 50.3 us -> 0 us
  starting transfers between devices: 0.85 us -> 21.1 us
  matrix products: 40.4 us -> 25.1 us
  local copies, waits for them, and re-layouts: 19.8 us -> 27.3 us
    ppermute x0 -> x23, waiting for transfers between devices: none -> 158 us  [the longest x12 148 us: shifted(): return lax.ppermute(rows, 'tensor', pairs)]
    reduce_scatter x5 -> x1, waiting for transfers between devices: 144 us -> 0.02 us  [shards(): lax.psum_scatter(wide_part, 'tensor', scatter_dimension=0, tiled=True)]
    all_gather x5 -> x3, waiting for transfers between devices: 148 us -> 29.4 us  [the longest x2 29.4 us: shards(): wide_full = lax.all_gather(lax.all_gather(wide_block, 'tensor'), 'chip')]
    psum x1 -> x0, blocking collectives: 38.9 us -> none  [shards(): lax.psum(jnp.concatenate([vector_grad, unit_grad.reshape(-1, model)], axi...]
    ppermute x0 -> x23, starting transfers between devices: none -> 20.9 us  [the longest x12 10.6 us: shifted(): return lax.ppermute(rows, 'tensor', pairs)]
    all_gather x1 -> x0, blocking collectives: 11.3 us -> none  [shards(): lax.all_gather(qkv_weight.reshape(-1, triple).astype(BF), 'fsdp', axis=0,...]
    dot_general x6, matrix products: 19.7 us -> 11.8 us  [contract(): lax.dot_general(left, right, (((left_dim,), (right_dim,)), ((), ())), pre...]
    slice x0 -> x6, local copies, waits for them, and re-layouts: none -> 5.45 us  [the longest x1 2.97 us: shards(): wide_full[:, place, :, start:start + half_width].reshape(model, half_width)]
  transfers between devices with their start and end apart: 11 -> 29, of which waited for: 10 -> 21; matrix products, arithmetic and copies ran while one was open for 9% -> 13% of each run, Pallas kernels for 4% -> 5%
where the time goes in v2:
time: 321 us; the launch traced here: 320 us
  waiting for transfers between devices  188 us (59%)
  local copies, waits for them, and re-layouts  27.3 us (9%)
  other arithmetic  25.5 us (8%)
  matrix products  25.1 us (8%)
  starting transfers between devices  21.1 us (7%)
  Pallas kernels  17.6 us (5%)
  between operations  15.3 us (5%)
    ppermute x12, waiting for transfers between devices, shifted(): return lax.ppermute(rows, 'tensor', pairs)  148 us
    all_gather x2, waiting for transfers between devices, shards(): wide_full = lax.all_gather(lax.all_gather(wide_block, 'tensor'), 'chip')  29.4 us
    unnamed x106, local copies, waits for them, and re-layouts  13.3 us
    pallas_call x1, Pallas kernels, attend_backward(): pl.pallas_call(attend_backward_kernel, grid=(count,), in_specs=[by_sequen...  12.6 us
    dot_general x6, matrix products, contract(): lax.dot_general(left, right, (((left_dim,), (right_dim,)), ((), ())), pre...  11.8 us
    ppermute x12, starting transfers between devices, shifted(): return lax.ppermute(rows, 'tensor', pairs)  10.6 us
    dot_general x1, matrix products, shards(): jnp.dot(first_whole, up_full, preferred_element_type=F32) + unit_slice  7.7 us
  transfers between devices with their start and end apart: 29, of which 21 were waited for; matrix products, arithmetic and copies ran while one was open for 13% of the time, Pallas kernels for 5%

profile of v2, /device:TPU:9, one launch (start us, length us, event | category | flops | bytes accessed | tf_op | source)
XLA Modules:
  0.0 319.9 jit_solution(1555161802964674295)
XLA Ops:
  13.9 29.4 %all-gather.7.cloned.1.call-done = bf16[4,192,768]{2,1,0:T(8,128)(2,1)} async-done(((bf16[1,192,768]{2,1,0:T(8,128)(2,1)}), bf16[4,192,768]{2,1,0:T(8,128)(2,1)}) %all-gather.7.cloned.1.call-update) | async-done | bytes 1179664 | tf_op jit(solution)/shard_map/all_gather | solution.py:295
  44.5 1.4 collective-permute-start.1
  46.5 6.7 %collective-permute-done = bf16[2,128,768]{2,1,0:T(8,128)(2,1)} collective-permute-done((bf16[2,128,768]{2,1,0:T(8,128)(2,1)S(1)}, bf16[2,128,768]{2,1,0:T(8,128)(2,1)}, u32[]{:S(2)}, u32[]{:S(2)}) %collective-permute-start) | collective-permute-done | bytes 393248 | tf_op jit(solution)/shard_map/ppermute | solution.py:229
  54.3 23.3 %collective-permute-done.1 = bf16[2,128,768]{2,1,0:T(8,128)(2,1)S(1)} collective-permute-done((bf16[2,128,768]{2,1,0:T(8,128)(2,1)S(1)}, bf16[2,128,768]{2,1,0:T(8,128)(2,1)S(1)}, u32[]{:S(2)}, u32[]{:S(2)}) %collective-permute-start.1) | collective-permute-done | bytes 393248 | tf_op jit(solution)/shard_map/ppermute | solution.py:229
  77.6 3.2 %collective-permute-done.2 = bf16[2,128,768]{2,1,0:T(8,128)(2,1)S(1)} collective-permute-done((bf16[2,128,768]{2,1,0:T(8,128)(2,1)S(1)}, bf16[2,128,768]{2,1,0:T(8,128)(2,1)S(1)}, u32[]{:S(2)}, u32[]{:S(2)}) %collective-permute-start.2) | collective-permute-done | bytes 393248 | tf_op jit(solution)/shard_map/ppermute | solution.py:229
  80.9 1.9 slice.160.weight_ref
  82.8 5.0 %attend_forward.1 = (bf16[2,512,576]{2,1,0:T(8,128)(2,1)S(1)}, bf16[2,512,192]{2,1,0:T(8,128)(2,1)S(1)}) custom-call(bf16[2,512,768]{2,1,0:T(8,128)(2,1)S(1)} %bitcast.175, bf16[768,576]{1,0:T(8,128)(2,1)S(1)} %slice.160.weight_ref, f32[1,576]{1,0:T(1,128)S(1)} %broadcast_in_dim.52.bias_ref, s32[2,512,1]{2,1,0:T(8,128)S(1)} %copy.150.down_ref, ...), custom_call_target="tpu_custom_call" | custom-call | tf_op jit(solution)/shard_map/attend_forward/pallas_call | solution.py:130
  87.8 2.0 convolution_convert_fusion.2
  91.1 1.5 collective-permute-start.5
  93.2 8.1 %collective-permute-done.3 = bf16[2,128,768]{2,1,0:T(8,128)(2,1)S(1)} collective-permute-done((bf16[2,128,768]{2,1,0:T(8,128)(2,1)S(1)}, bf16[2,128,768]{2,1,0:T(8,128)(2,1)S(1)}, u32[]{:S(2)}, u32[]{:S(2)}) %collective-permute-start.3) | collective-permute-done | bytes 393248 | tf_op jit(solution)/shard_map/ppermute | solution.py:229
  101.3 23.4 %collective-permute-done.4 = bf16[2,128,768]{2,1,0:T(8,128)(2,1)} collective-permute-done((bf16[2,128,768]{2,1,0:T(8,128)(2,1)S(1)}, bf16[2,128,768]{2,1,0:T(8,128)(2,1)}, u32[]{:S(2)}, u32[]{:S(2)}) %collective-permute-start.4) | collective-permute-done | bytes 393248 | tf_op jit(solution)/shard_map/ppermute | solution.py:229
  126.0 1.6 add_reduce_fusion
  128.8 3.0 fusion.57
  131.8 7.7 %multiply_convert_fusion = (bf16[512,1536]{1,0:T(8,128)(2,1)S(1)}, f32[512,1536]{1,0:T(8,128)S(1)}, f32[512,1536]{1,0:T(8,128)S(1)}) fusion(f32[1536]{0:T(1024)S(1)} %add.315, bf16[768,384]{1,0:T(8,128)(2,1)S(1)} %bitcast.197, bf16[768,384]{1,0:T(8,128)(2,1)S(1)} %bitcast.199, bf16[768,384]{1,0:T(8,128)(2,1)S(1)} %bitcast.201, ...), kind=kOutput, calls=%fused_computation.8 | convolution fusion | flops 1270874112 | bytes 11016192 | tf_op jit(solution)/shard_map/dot_general | solution.py:316
  144.6 1.7 fusion.45
  149.0 3.9 %convert_reduce_fusion = (f32[1536]{0:T(1024)}, bf16[512,1536]{1,0:T(8,128)(2,1)S(1)}) fusion(f32[512,1536]{1,0:T(8,128)S(1)} %get-tuple-element.150, f32[512,1536]{1,0:T(8,128)S(1)} %get-tuple-element.188, bf16[768,384]{1,0:T(8,128)(2,1)S(1)} %bitcast.208, bf16[768,384]{1,0:T(8,128)(2,1)S(1)} %bitcast.210, bf16[768,384]{1,0:T(8,128)(2,1)S(1)} %bitcast.212, ...), kind=kOutput, calls=%fused_computation.6 | convolution fusion | flops 1231550976 | bytes 11016192 | tf_op jit(solution)/shard_map/dot_general | solution.py:327
  156.6 2.4 pad_maximum_fusion
  159.1 3.5 %fusion.26 = f32[512,768]{1,0:T(8,128)S(1)} fusion(bf16[512,1536]{1,0:T(8,128)(2,1)} %copy-done.45, bf16[768,384]{1,0:T(8,128)(2,1)} %bitcast.198, bf16[768,384]{1,0:T(8,128)(2,1)} %bitcast.200, bf16[768,384]{1,0:T(8,128)(2,1)} %bitcast.202, bf16[768,384]{1,0:T(8,128)(2,1)} %bitcast.204), kind=kOutput, calls=%fused_computation.79 | convolution fusion | flops 1217396736 | bytes 5505024 | tf_op jit(solution)/shard_map/dot_general | solution.py:22
  170.5 6.6 %collective-permute-done.11 = bf16[2,128,768]{2,1,0:T(8,128)(2,1)S(1)} collective-permute-done((bf16[2,128,768]{2,1,0:T(8,128)(2,1)S(1)}, bf16[2,128,768]{2,1,0:T(8,128)(2,1)S(1)}, u32[]{:S(2)}, u32[]{:S(2)}) %collective-permute-start.11) | collective-permute-done | bytes 393248 | tf_op jit(solution)/shard_map/ppermute | solution.py:229
  177.1 24.2 %collective-permute-done.12 = bf16[2,128,768]{2,1,0:T(8,128)(2,1)S(1)} collective-permute-done((bf16[2,128,768]{2,1,0:T(8,128)(2,1)S(1)}, bf16[2,128,768]{2,1,0:T(8,128)(2,1)S(1)}, u32[]{:S(2)}, u32[]{:S(2)}) %collective-permute-start.12) | collective-permute-done | bytes 393248 | tf_op jit(solution)/shard_map/ppermute | solution.py:229
  201.3 2.7 collective-permute-done.13
  205.2 1.8 convolution_convert_fusion.3
  207.2 1.9 convolution_convert_fusion.4
  210.7 12.6 %attend_backward.1 = (bf16[2,512,768]{2,1,0:T(8,128)(2,1)S(1)}, f32[768,576]{1,0:T(8,128)}, f32[1,576]{1,0:T(1,128)S(1)}) custom-call(bf16[2,512,768]{2,1,0:T(8,128)(2,1)} %bitcast.176, bf16[768,576]{1,0:T(8,128)(2,1)S(1)} %slice.160.weight_ref, bf16[2,512,576]{2,1,0:T(8,128)(2,1)S(1)} %copy-done.4, bf16[2,512,192]{2,1,0:T(8,128)(2,1)S(1)} %bitcast.177, ...), custom_call_target="tpu_custom_call" | custom-call | tf_op jit(solution)/shard_map/attend_backward/pallas_call | solution.py:154
  224.4 1.6 convert.38
  231.2 1.8 collective-permute-done.19
  234.2 1.8 collective-permute-done.20
  243.7 2.1 collective-permute-start.15
  248.6 3.9 %collective-permute-done.14 = bf16[2,128,768]{2,1,0:T(8,128)(2,1)} collective-permute-done((bf16[2,128,768]{2,1,0:T(8,128)(2,1)}, bf16[2,128,768]{2,1,0:T(8,128)(2,1)}, u32[]{:S(2)}, u32[]{:S(2)}) %collective-permute-start.14) | collective-permute-done | bytes 393248 | tf_op jit(solution)/shard_map/ppermute | solution.py:229
  252.4 36.9 %collective-permute-done.15 = bf16[2,128,768]{2,1,0:T(8,128)(2,1)} collective-permute-done((bf16[2,128,768]{2,1,0:T(8,128)(2,1)}, bf16[2,128,768]{2,1,0:T(8,128)(2,1)}, u32[]{:S(2)}, u32[]{:S(2)}) %collective-permute-start.15) | collective-permute-done | bytes 393248 | tf_op jit(solution)/shard_map/ppermute | solution.py:229
  289.3 7.8 %collective-permute-done.16 = bf16[2,128,768]{2,1,0:T(8,128)(2,1)} collective-permute-done((bf16[2,128,768]{2,1,0:T(8,128)(2,1)}, bf16[2,128,768]{2,1,0:T(8,128)(2,1)}, u32[]{:S(2)}, u32[]{:S(2)}) %collective-permute-start.16) | collective-permute-done | bytes 393248 | tf_op jit(solution)/shard_map/ppermute | solution.py:229
  305.0 3.4 %collective-permute-start.17 = (bf16[96,2,384]{2,0,1:T(8,128)(2,1)S(1)}, bf16[96,2,384]{2,0,1:T(8,128)(2,1)S(1)}, u32[]{:S(2)}, u32[]{:S(2)}) collective-permute-start(bf16[96,2,384]{2,0,1:T(8,128)(2,1)S(1)} %bitcast.215), channel_id=1, source_target_pairs={{0,4},{4,0},{1,5},{5,1},{2,6},{6,2},{3,7},{7,3},{8,12},{12,8},{9,1... | collective-permute-start | bytes 442376 | tf_op jit(solution)/shard_map/ppermute | solution.py:250
  (257 shorter events, 65.9 us)
Async XLA Ops:
  7.2 36.1 %all-gather.7.cloned.1.call-start = ((), (), s32[]{:S(2)}) async-start(), calls=%async_computation.4 | async-start | bytes 1474560 | tf_op jit(solution)/shard_map/all_gather | solution.py:295
  9.5 1.7 collective-permute-start.7
  12.6 68.3 %all-gather.5.cloned.1.call-start = ((), (), s32[]{:S(2)}) async-start(), calls=%async_computation.3 | async-start | bytes 1327104 | tf_op jit(solution)/shard_map/all_gather | solution.py:286
  13.9 114.9 %all-gather.9.cloned.1.call-start = ((), (), s32[]{:S(2)}) async-start(), calls=%async_computation.7 | async-start | bytes 5898240 | tf_op jit(solution)/shard_map/all_gather | solution.py:295
  43.3 184.2 %reduce-scatter.10.cloned.1.call-start = ((), (), s32[]{:S(2)}) async-start(), calls=%async_computation.8 | async-start | bytes 5898240
  43.4 9.9 %collective-permute-start = (bf16[2,128,768]{2,1,0:T(8,128)(2,1)S(1)}, bf16[2,128,768]{2,1,0:T(8,128)(2,1)}, u32[]{:S(2)}, u32[]{:S(2)}) collective-permute-start(bf16[2,128,768]{2,1,0:T(8,128)(2,1)S(1)} %copy-done.14), channel_id=1, source_target_pairs={{0,1},{1,2},{2,3},{3,0},{4,5},{5,6},{6,7},{7,4},{8,9},{9,10},{10,1... | collective-permute-start | bytes 1179656 | tf_op jit(solution)/shard_map/ppermute | solution.py:229
  44.5 33.1 %collective-permute-start.1 = (bf16[2,128,768]{2,1,0:T(8,128)(2,1)S(1)}, bf16[2,128,768]{2,1,0:T(8,128)(2,1)S(1)}, u32[]{:S(2)}, u32[]{:S(2)}) collective-permute-start(bf16[2,128,768]{2,1,0:T(8,128)(2,1)S(1)} %copy-done.14), channel_id=1, source_target_pairs={{0,2},{1,3},{2,0},{3,1},{4,6},{5,7},{6,4},{7,5},{8,10},{9,11},{10,... | collective-permute-start | bytes 1179656 | tf_op jit(solution)/shard_map/ppermute | solution.py:229
  45.9 34.9 %collective-permute-start.2 = (bf16[2,128,768]{2,1,0:T(8,128)(2,1)S(1)}, bf16[2,128,768]{2,1,0:T(8,128)(2,1)S(1)}, u32[]{:S(2)}, u32[]{:S(2)}) collective-permute-start(bf16[2,128,768]{2,1,0:T(8,128)(2,1)S(1)} %copy-done.14), channel_id=1, source_target_pairs={{0,3},{1,0},{2,1},{3,2},{4,7},{5,4},{6,5},{7,6},{8,11},{9,8},{10,9... | collective-permute-start | bytes 1179656 | tf_op jit(solution)/shard_map/ppermute | solution.py:229
  89.9 38.7 %copy-start.35 = (f32[3072]{0:T(1024)S(1)}, f32[3072]{0:T(1024)}, u32[]{:S(2)}) copy-start(f32[3072]{0:T(1024)} %param.39) | copy-start | bytes 36868
  91.1 10.2 %collective-permute-start.3 = (bf16[2,128,768]{2,1,0:T(8,128)(2,1)S(1)}, bf16[2,128,768]{2,1,0:T(8,128)(2,1)S(1)}, u32[]{:S(2)}, u32[]{:S(2)}) collective-permute-start(bf16[2,128,768]{2,1,0:T(8,128)(2,1)S(1)} %get-tuple-element.172), channel_id=1, source_target_pairs={{0,1},{1,2},{2,3},{3,0},{4,5},{5,6},{6,7},{7,4},{8,9},{9,10},{10,1... | collective-permute-start | bytes 1179656 | tf_op jit(solution)/shard_map/ppermute | solution.py:229
  91.1 33.6 %collective-permute-start.4 = (bf16[2,128,768]{2,1,0:T(8,128)(2,1)S(1)}, bf16[2,128,768]{2,1,0:T(8,128)(2,1)}, u32[]{:S(2)}, u32[]{:S(2)}) collective-permute-start(bf16[2,128,768]{2,1,0:T(8,128)(2,1)S(1)} %get-tuple-element.174), channel_id=1, source_target_pairs={{0,2},{1,3},{2,0},{3,1},{4,6},{5,7},{6,4},{7,5},{8,10},{9,11},{10,... | collective-permute-start | bytes 1179656 | tf_op jit(solution)/shard_map/ppermute | solution.py:229
  91.1 34.9 %collective-permute-start.5 = (bf16[2,128,768]{2,1,0:T(8,128)(2,1)S(1)}, bf16[2,128,768]{2,1,0:T(8,128)(2,1)}, u32[]{:S(2)}, u32[]{:S(2)}) collective-permute-start(bf16[2,128,768]{2,1,0:T(8,128)(2,1)S(1)} %get-tuple-element.173), channel_id=1, source_target_pairs={{0,3},{1,0},{2,1},{3,2},{4,7},{5,4},{6,5},{7,6},{8,11},{9,8},{10,9... | collective-permute-start | bytes 1179656 | tf_op jit(solution)/shard_map/ppermute | solution.py:229
  128.1 3.7 %collective-permute-start.6 = (bf16[256,768]{1,0:T(8,128)(2,1)S(1)}, bf16[256,768]{1,0:T(8,128)(2,1)S(1)}, u32[]{:S(2)}, u32[]{:S(2)}) collective-permute-start(bf16[256,768]{1,0:T(8,128)(2,1)S(1)} %fusion.23), channel_id=1, source_target_pairs={{0,4},{4,0},{1,5},{5,1},{2,6},{6,2},{3,7},{7,3},{8,12},{12,8},{9,1... | collective-permute-start | bytes 1179656 | tf_op jit(solution)/shard_map/ppermute | solution.py:250
  141.0 2.0 collective-permute-start.8
  147.2 1.8 collective-permute-start.9
  159.1 140.5 %reduce-scatter.6.cloned.1.call-start = ((), (), s32[]{:S(2)}) async-start(), calls=%async_computation.5 | async-start | bytes 1327104 | tf_op jit(solution)/shard_map/reduce_scatter | solution.py:357
  162.7 1.8 collective-permute-start.10
  166.6 10.5 %collective-permute-start.11 = (bf16[2,128,768]{2,1,0:T(8,128)(2,1)S(1)}, bf16[2,128,768]{2,1,0:T(8,128)(2,1)S(1)}, u32[]{:S(2)}, u32[]{:S(2)}) collective-permute-start(bf16[2,128,768]{2,1,0:T(8,128)(2,1)S(1)} %bitcast.190), channel_id=1, source_target_pairs={{0,1},{1,2},{2,3},{3,0},{4,5},{5,6},{6,7},{7,4},{8,9},{9,10},{10,1... | collective-permute-start | bytes 1179656 | tf_op jit(solution)/shard_map/ppermute | solution.py:229
  167.9 33.4 %collective-permute-start.12 = (bf16[2,128,768]{2,1,0:T(8,128)(2,1)S(1)}, bf16[2,128,768]{2,1,0:T(8,128)(2,1)S(1)}, u32[]{:S(2)}, u32[]{:S(2)}) collective-permute-start(bf16[2,128,768]{2,1,0:T(8,128)(2,1)S(1)} %bitcast.191), channel_id=1, source_target_pairs={{0,2},{1,3},{2,0},{3,1},{4,6},{5,7},{6,4},{7,5},{8,10},{9,11},{10,... | collective-permute-start | bytes 1179656 | tf_op jit(solution)/shard_map/ppermute | solution.py:229
  169.0 35.0 %collective-permute-start.13 = (bf16[2,128,768]{2,1,0:T(8,128)(2,1)S(1)}, bf16[2,128,768]{2,1,0:T(8,128)(2,1)S(1)}, u32[]{:S(2)}, u32[]{:S(2)}) collective-permute-start(bf16[2,128,768]{2,1,0:T(8,128)(2,1)S(1)} %bitcast.192), channel_id=1, source_target_pairs={{0,3},{1,0},{2,1},{3,2},{4,7},{5,4},{6,5},{7,6},{8,11},{9,8},{10,9... | collective-permute-start | bytes 1179656 | tf_op jit(solution)/shard_map/ppermute | solution.py:229
  170.5 36.7 %copy-start.6 = (bf16[2,512,192]{2,1,0:T(8,128)(2,1)S(1)}, bf16[2,512,192]{2,1,0:T(8,128)(2,1)}, u32[]{:S(2)}) copy-start(bf16[2,512,192]{2,1,0:T(8,128)(2,1)} %copy-done.5) | copy-start | bytes 1179652
  227.5 76.2 %reduce-scatter.8.cloned.1.call-start = ((), (), s32[]{:S(2)}) async-start(), calls=%async_computation.6 | async-start | bytes 1474560 | tf_op jit(solution)/shard_map/reduce_scatter | solution.py:344
  228.6 1.4 collective-permute-start.18
  230.0 3.0 collective-permute-start.19
  233.0 3.0 collective-permute-start.20
  236.6 3.3 %collective-permute-start.21 = (f32[12,768]{1,0:T(8,128)}, f32[12,768]{1,0:T(8,128)}, u32[]{:S(2)}, u32[]{:S(2)}) collective-permute-start(f32[12,768]{1,0:T(8,128)} %add.355), channel_id=1, source_target_pairs={{0,1},{1,0},{2,3},{3,2},{4,5},{5,4},{6,7},{7,6},{8,9},{9,8},{10,11... | collective-permute-start | bytes 110600 | tf_op jit(solution)/shard_map/ppermute | solution.py:272
  236.9 61.6 %copy-start.8 = (f32[256,768]{1,0:T(8,128)S(1)}, f32[256,768]{1,0:T(8,128)}, u32[]{:S(2)}) copy-start(f32[256,768]{1,0:T(8,128)} %copy-done.7) | copy-start | bytes 2359300
  240.7 5.1 %collective-permute-start.22 = (f32[12,768]{1,0:T(8,128)S(1)}, f32[12,768]{1,0:T(8,128)S(1)}, u32[]{:S(2)}, u32[]{:S(2)}) collective-permute-start(f32[12,768]{1,0:T(8,128)S(1)} %add.356), channel_id=1, source_target_pairs={{0,2},{1,3},{2,0},{3,1},{4,6},{5,7},{6,4},{7,5},{8,10},{9,11},{10,... | collective-permute-start | bytes 110600 | tf_op jit(solution)/shard_map/ppermute | solution.py:272
  242.9 9.5 %collective-permute-start.14 = (bf16[2,128,768]{2,1,0:T(8,128)(2,1)}, bf16[2,128,768]{2,1,0:T(8,128)(2,1)}, u32[]{:S(2)}, u32[]{:S(2)}) collective-permute-start(bf16[2,128,768]{2,1,0:T(8,128)(2,1)} %get-tuple-element.169), channel_id=1, source_target_pairs={{0,1},{1,2},{2,3},{3,0},{4,5},{5,6},{6,7},{7,4},{8,9},{9,10},{10,1... | collective-permute-start | bytes 1179656 | tf_op jit(solution)/shard_map/ppermute | solution.py:229
  243.7 45.6 %collective-permute-start.15 = (bf16[2,128,768]{2,1,0:T(8,128)(2,1)}, bf16[2,128,768]{2,1,0:T(8,128)(2,1)}, u32[]{:S(2)}, u32[]{:S(2)}) collective-permute-start(bf16[2,128,768]{2,1,0:T(8,128)(2,1)} %get-tuple-element.171), channel_id=1, source_target_pairs={{0,2},{1,3},{2,0},{3,1},{4,6},{5,7},{6,4},{7,5},{8,10},{9,11},{10,... | collective-permute-start | bytes 1179656 | tf_op jit(solution)/shard_map/ppermute | solution.py:229
  245.8 51.4 %collective-permute-start.16 = (bf16[2,128,768]{2,1,0:T(8,128)(2,1)}, bf16[2,128,768]{2,1,0:T(8,128)(2,1)}, u32[]{:S(2)}, u32[]{:S(2)}) collective-permute-start(bf16[2,128,768]{2,1,0:T(8,128)(2,1)} %get-tuple-element.170), channel_id=1, source_target_pairs={{0,3},{1,0},{2,1},{3,2},{4,7},{5,4},{6,5},{7,6},{8,11},{9,8},{10,9... | collective-permute-start | bytes 1179656 | tf_op jit(solution)/shard_map/ppermute | solution.py:229
  305.0 5.7 %collective-permute-start.17 = (bf16[96,2,384]{2,0,1:T(8,128)(2,1)S(1)}, bf16[96,2,384]{2,0,1:T(8,128)(2,1)S(1)}, u32[]{:S(2)}, u32[]{:S(2)}) collective-permute-start(bf16[96,2,384]{2,0,1:T(8,128)(2,1)S(1)} %bitcast.215), channel_id=1, source_target_pairs={{0,4},{4,0},{1,5},{5,1},{2,6},{6,2},{3,7},{7,3},{8,12},{12,8},{9,1... | collective-permute-start | bytes 442376 | tf_op jit(solution)/shard_map/ppermute | solution.py:250
  (44 other events, 361.5 us)
Sparse Core Ops, SparseCore 0:
  12.7 30.5 all-gather.6
  45.8 24.3 all-gather.4
  72.0 56.6 all-gather.8
  159.2 57.5 reduce-scatter.9
  227.6 35.5 reduce-scatter.5
  265.4 36.2 reduce-scatter.7
